TPU v7x, 32 devices: a whole 2x2x4 slice. The times are simulated.
32 devices in a mesh: dom: 32 (over z, y, x, core).
Axes of the slice: x: 2, y: 2, z: 4, core: 2. Of those that a mesh axis runs over, the one named last changes fastest.
Arguments:
- coefficients: float32 [32, 27, 3, 3, 8, 128], P('dom'), may hold values from -11 to 11
- sketch: float32 [32, 3, 64, 8, 128], P('dom'), may hold values from -10 to 10
Outputs:
- basis_out: float32 [32, 3, 64, 8, 128], P('dom')
- factor: float32 [64, 64], replicated
All inputs are finite; a program needn't handle non-finite values.
Results may differ from a plain program's by a relative error of at most 0.0003.
Values sent between devices are 32-bit elements; how exact they have to be, the bound alone decides.
No kernel may reach another device: no remote copies, remote signals or barrier semaphores. Data moves between devices by JAX's collectives and lax.ppermute only.
A program may use at most 64 MiB of HBM per device.

v0:
```python
import jax
import jax.numpy as jnp
from jax import lax
from jax.sharding import PartitionSpec as P


def padded_2(cells, sides, width):
    for axis, dim in sides:
        count = lax.axis_size(axis)
        ends = count - 1
        head = lax.slice_in_dim(cells, 0, width, axis=dim)
        tail = lax.slice_in_dim(cells, cells.shape[dim] - width, cells.shape[dim], axis=dim)
        cells = jnp.concatenate(
            [
                lax.ppermute(tail, axis, [(i, (i + 1) % count) for i in range(ends)]),
                cells,
                lax.ppermute(head, axis, [((i + 1) % count, i) for i in range(ends)]),
            ],
            axis=dim,
        )
    return cells


def apply_blocks(padded, coefficients):
    planes = coefficients.shape[0]
    rows_y = coefficients.shape[4]
    cols_z = coefficients.shape[5]
    accum = jnp.zeros((planes, 3, padded.shape[2], rows_y, cols_z), jnp.float32)
    for shift_x in range(3):
        for shift_y in range(3):
            for shift_z in range(3):
                offset_index = shift_x * 9 + shift_y * 3 + shift_z
                window = padded[
                    shift_x : shift_x + planes,
                    :,
                    :,
                    shift_y : shift_y + rows_y,
                    shift_z : shift_z + cols_z,
                ]
                for source in range(3):
                    accum = (
                        accum
                        + coefficients[:, offset_index, :, source][:, :, None]
                        * window[:, source][:, None]
                    )
    return accum


def upper_factor(gram_matrix):
    order = gram_matrix.shape[0]
    positions = jnp.arange(order, dtype=jnp.int32)

    def column_step(column, lower):
        row_part = lax.dynamic_index_in_dim(lower, column, 0, keepdims=False)
        target = lax.dynamic_index_in_dim(gram_matrix, column, 1, keepdims=False)
        remain = target - jnp.dot(
            lower, row_part, precision=lax.Precision.HIGHEST, preferred_element_type=jnp.float32
        )
        pivot = jnp.sqrt(lax.dynamic_index_in_dim(remain, column, 0, keepdims=False))
        new_column = jnp.where(positions >= column, remain / pivot, jnp.zeros_like(remain))
        return lax.dynamic_update_index_in_dim(lower, new_column, column, 1)

    lower = lax.fori_loop(0, order, column_step, jnp.zeros_like(gram_matrix))
    return lower.T


def upper_inverse(upper_part):
    order = upper_part.shape[0]
    identity = jnp.eye(order, dtype=upper_part.dtype)

    def row_step(count, solved):
        row = order - 1 - count
        upper_row = lax.dynamic_index_in_dim(upper_part, row, 0, keepdims=False)
        unit_row = lax.dynamic_index_in_dim(identity, row, 0, keepdims=False)
        pivot = lax.dynamic_index_in_dim(upper_row, row, 0, keepdims=False)
        known = jnp.dot(
            upper_row, solved, precision=lax.Precision.HIGHEST, preferred_element_type=jnp.float32
        )
        return lax.dynamic_update_index_in_dim(solved, (unit_row - known) / pivot, row, 0)

    return lax.fori_loop(0, order, row_step, jnp.zeros_like(upper_part))


def shards(coefficients, sketch):
    slab_ext = padded_2(sketch, (("dom", 0),), 1)
    padded = jnp.pad(slab_ext, ((0, 0), (0, 0), (0, 0), (1, 1), (1, 1)))
    applied = apply_blocks(padded, coefficients)
    total_rows = 3.0 * lax.axis_size("dom") * sketch.shape[0] * sketch.shape[3] * sketch.shape[4]
    gram_local = (
        jnp.einsum("xakyz,xalyz->kl", applied, applied, precision=lax.Precision.HIGHEST)
        / total_rows
    )
    gram_total = lax.psum(gram_local, "dom")
    factor = upper_factor(gram_total)
    inverse = upper_inverse(factor)
    basis_out = jnp.einsum("xalyz,lk->xakyz", applied, inverse, precision=lax.Precision.HIGHEST)
    return (basis_out, factor)


def solution(mesh):
    placed = (P("dom", None, None, None, None, None), P("dom", None, None, None, None))
    return jax.shard_map(
        shards,
        mesh=mesh,
        in_specs=placed,
        out_specs=(P("dom", None, None, None, None), P()),
        check_vma=False,
    )
```

profile of v0, /device:TPU:0, one launch (start us, length us, event | category | flops | bytes accessed | tf_op | source)
XLA Modules:
  0.0 347.4 jit_solution(4483302255161633557)
XLA Ops:
  0.6 2.4 collective-permute-start
  4.3 1.6 slice_bitcast_fusion.161
  9.3 1.6 slice_bitcast_fusion.160
  10.9 1.6 slice_bitcast_fusion.159
  12.5 1.6 slice_bitcast_fusion.158
  14.2 5.4 %select_maximum_fusion = f32[3,3,64,10,130]{4,3,2,1,0:T(8,128)S(1)} fusion(f32[1,3,64,8,128]{4,3,2,1,0:T(8,128)S(1)} %collective-permute-done.1, f32[1,3,64,8,128]{4,3,2,1,0:T(8,128)} %param.7, f32[1,3,64,8,128]{4,3,2,1,0:T(8,128)S(1)} %collective-permute-done), kind=kLoop, calls=%fused_computation.19 | loop fusion | flops 11232000 | bytes 5354496 | tf_op jit(solution)/shard_map/concatenate | solution.py:13
  20.6 2.9 slice_bitcast_fusion.76
  23.4 2.6 slice_bitcast_fusion.77
  33.0 11.4 %multiply_add_fusion = f32[3,64,8,128]{3,1,2,0:T(8,128)S(1)} fusion(f32[64,8,128]{2,0,1:T(8,128)S(1)} %copy.85, f32[3,8,128]{2,1,0:T(8,128)S(1)} %copy-done.40, f32[64,8,128]{2,0,1:T(8,128)S(1)} %copy.84, f32[3,8,128]{2,1,0:T(8,128)S(1)} %copy-done.41, f32[64,8,128]{2,0,1:T(8,128)S(1)} %copy.83, f32[3,8,128]{2,1,0:T(8,128)S(1)} %get-tuple-element.310, ...), kind=kLoop, calls=%fused_computation.27 | loop fusion | flops 31653888 | bytes 23015424 | tf_op jit(solution)/shard_map/add | solution.py:42
  45.2 49.8 %psum.7 = f32[64,64]{1,0:T(8,128)S(1)} all-reduce(f32[64,64]{1,0:T(8,128)S(1)} %fusion.16), channel_id=1, replica_groups=mesh['dom'=32] {'dom'}, use_global_device_ids=true, to_apply=%region_0.1 | all-reduce | flops 4096 | bytes 32768 | tf_op jit(solution)/shard_map/psum | solution.py:93
  95.1 114.9 %while.31 = (s32[]{:T(128)}, f32[64,64]{1,0:T(8,128)S(1)}, f32[64,64]{0,1:T(8,128)S(1)}, s32[]{:T(128)}, s32[]{:T(128)}) while((s32[]{:T(128)}, f32[64,64]{1,0:T(8,128)S(1)}, f32[64,64]{0,1:T(8,128)S(1)}, s32[]{:T(128)}, s32[]{:T(128)}) %tuple.221), condition=%wide.region_2.3_spmd.clone, body=%wide.region_1.2_spmd.clone.sunk | while | flops 49410 | bytes 36701 | solution.py:63
  210.1 135.1 %while.30 = (s32[]{:T(128)}, f32[64,64]{1,0:T(8,128)S(1)}, f32[64,64]{1,0:T(8,128)}, f32[64,64]{1,0:T(8,128)S(1)}, s32[]{:T(128)}, /*index=5*/s32[]{:T(128)}, s32[]{:T(128)}, s32[]{:T(128)}) while((s32[]{:T(128)}, f32[64,64]{1,0:T(8,128)S(1)}, f32[64,64]{1,0:T(8,128)}, f32[64,64]{1,0:T(8,128)S(1)}, s32[]{:T(128)}, /*index=5*/s32[]{:T(128)}, ...), condition=%wide.region_4.5_spmd, body=%wide.region_3.4_spmd.sunk | while | flops 49287 | bytes 35495 | solution.py:81
  210.7 1.5 fusion.33
  212.8 1.5 fusion.33
  214.9 1.5 fusion.33
  217.0 1.5 fusion.33
  219.2 1.5 fusion.33
  221.3 1.5 fusion.33
  223.4 1.5 fusion.33
  225.5 1.5 fusion.33
  227.6 1.5 fusion.33
  229.7 1.5 fusion.33
  231.8 1.5 fusion.33
  233.9 1.5 fusion.33
  236.0 1.5 fusion.33
  238.2 1.5 fusion.33
  240.3 1.5 fusion.33
  242.4 1.5 fusion.33
  244.5 1.5 fusion.33
  246.6 1.5 fusion.33
  248.7 1.5 fusion.33
  250.8 1.5 fusion.33
  267.7 1.5 fusion.33
  269.8 1.5 fusion.33
  271.9 1.5 fusion.33
  274.1 1.5 fusion.33
  276.2 1.5 fusion.33
  278.3 1.5 fusion.33
  280.4 1.5 fusion.33
  282.5 1.5 fusion.33
  307.8 1.5 fusion.33
  309.9 1.5 fusion.33
  312.1 1.5 fusion.33
  314.2 1.5 fusion.33
  316.3 1.5 fusion.33
  318.4 1.5 fusion.33
  320.5 1.5 fusion.33
  322.6 1.5 fusion.33
  (716 shorter events, 162.9 us)
Async XLA Ops:
  0.6 13.5 %collective-permute-start = (f32[1,3,64,8,128]{4,3,2,1,0:T(8,128)}, f32[1,3,64,8,128]{4,3,2,1,0:T(8,128)S(1)}, u32[]{:S(2)}, u32[]{:S(2)}) collective-permute-start(f32[1,3,64,8,128]{4,3,2,1,0:T(8,128)} %param.7), channel_id=1, source_target_pairs={{0,1},{1,2},{2,3},{3,4},{4,5},{5,6},{6,7},{7,8},{8,9},{9,10},{10,1... | collective-permute-start | bytes 2359304 | tf_op jit(solution)/shard_map/ppermute | solution.py:15
  3.0 11.1 %collective-permute-start.1 = (f32[1,3,64,8,128]{4,3,2,1,0:T(8,128)}, f32[1,3,64,8,128]{4,3,2,1,0:T(8,128)S(1)}, u32[]{:S(2)}, u32[]{:S(2)}) collective-permute-start(f32[1,3,64,8,128]{4,3,2,1,0:T(8,128)} %param.7), channel_id=1, source_target_pairs={{1,0},{2,1},{3,2},{4,3},{5,4},{6,5},{7,6},{8,7},{9,8},{10,9},{11,1... | collective-permute-start | bytes 2359304 | tf_op jit(solution)/shard_map/ppermute | solution.py:17
  26.0 2.4 copy-start.27
  26.0 2.5 copy-start.26
  26.0 2.6 copy-start.25
  26.1 2.6 copy-start.24
  26.1 2.7 copy-start.23
  26.1 2.7 copy-start.22
  26.1 2.8 copy-start.21
  26.9 2.4 copy-start.15
  27.0 2.4 copy-start.14
  27.0 2.5 copy-start.13
  27.0 2.5 copy-start.11
  27.1 2.5 copy-start.12
  27.2 2.5 copy-start.10
  27.2 2.5 copy-start.9
  27.3 2.5 copy-start.8
  27.4 2.5 copy-start.7
  27.5 2.5 copy-start.6
  27.6 2.5 copy-start.5
  27.7 2.5 copy-start.4
  27.7 2.5 copy-start.3
  27.8 2.5 copy-start.2
  27.9 2.9 copy-start.1
  27.9 2.9 copy-start
  30.3 2.4 copy-start.30
  30.3 2.4 copy-start.31
  30.3 2.4 copy-start.32
  30.3 2.4 copy-start.33
  30.3 2.4 copy-start.34
  30.3 2.4 copy-start.35
  30.4 2.4 copy-start.36
  30.4 2.4 copy-start.37
  30.4 2.4 copy-start.38
  30.4 2.4 copy-start.39
  30.4 2.4 copy-start.40
  30.4 2.4 copy-start.41
  30.4 2.4 copy-start.42
  30.4 2.4 copy-start.43
  30.4 2.4 copy-start.44
  30.4 2.4 copy-start.45
  30.5 2.4 copy-start.46
  30.5 2.4 copy-start.47
  30.5 2.4 copy-start.48
  30.5 2.4 copy-start.49
  30.5 2.4 copy-start.50
  30.5 2.4 copy-start.51
  30.5 2.4 copy-start.52
  (25 other events, 56.7 us)
where the time goes:
time: 351 us; the launch traced here: 347 us
  local copies, waits for them, and re-layouts  121 us (34%)
  matrix products  105 us (30%)
  blocking collectives  49.8 us (14%)
  loops' own time  48.3 us (14%)
  other arithmetic  17.8 us (5%)
  starting transfers between devices  3.7 us (1%)
    dot_general x64, matrix products, row_step(): jnp.dot(upper_row, solved, precision=lax.Precision.HIGHEST, preferred_ele...  93.9 us
    psum x1, blocking collectives, shards(): gram_total = lax.psum(gram_local, 'dom')  49.8 us
    another operation x1, loops' own time, upper_factor(): lower = lax.fori_loop(0, order, column_step, jnp.zeros_like(gram_matrix))  46.3 us
    dynamic_slice x64, local copies, waits for them, and re-layouts, column_step(): lax.dynamic_index_in_dim(remain, column, 0, keepdims=False)  39.6 us
    dynamic_slice x64, local copies, waits for them, and re-layouts, row_step(): pivot = lax.dynamic_index_in_dim(upper_row, row, 0, keepdims=False)  37.7 us
    mul x93, local copies, waits for them, and re-layouts, apply_blocks(): coefficients[:, offset_index, :, source][:, :, None]  20.5 us
    dynamic_update_slice x64, local copies, waits for them, and re-layouts, column_step(): return lax.dynamic_update_index_in_dim(lower, new_column, column, 1)  13.3 us
    add x1, other arithmetic, apply_blocks(): accum + coefficients[:, offset_index, :, source][:, :, None] * window[:,...  11.4 us
  transfers between devices with their start and end apart: 2, of which 0 were waited for; matrix products, arithmetic and copies ran while one was open for 3% of the time, Pallas kernels for 0%

commit v1 on v0

v1 whole, which is shorter than its diff:
```python
import jax
import jax.numpy as jnp
from jax import lax
from jax.experimental import pallas as pl
from jax.experimental.pallas import tpu as pltpu
from jax.sharding import PartitionSpec as P

GROUP = 4
VMEM_LIMIT = 48 * 1024 * 1024


def iota(shape, dim):
    return lax.broadcasted_iota(jnp.int32, shape, dim)


def side_bases():
    odd = lax.axis_index("dom") % 2
    return (1 - odd) * 18, odd * 18


def prepare(coef_ref, out_ref, base, first, keep):
    rows_y, cols_z = coef_ref.shape[3:]
    sub = iota((rows_y, cols_z), 0)
    lane = iota((rows_y, cols_z), 1)
    for dy in range(3):
        for dz in range(3):
            valid = None
            if dy == 0:
                valid = sub < rows_y - 1
            elif dy == 2:
                valid = sub > 0
            edge = None
            if dz == 0:
                edge = lane > 0
            elif dz == 2:
                edge = lane < cols_z - 1
            for a in range(3):
                for b in range(3):
                    block = coef_ref[base + dy * 3 + dz, a, b]
                    if dy == 0:
                        block = pltpu.roll(block, rows_y - 1, 0)
                    elif dy == 2:
                        block = pltpu.roll(block, 1, 0)
                    mask = valid
                    if edge is not None:
                        mask = edge if mask is None else mask & edge
                    if keep is not None:
                        mask = keep if mask is None else mask & keep
                    if mask is not None:
                        block = jnp.where(mask, block, 0.0)
                    out_ref[first + dy * 3 + dz, a, b] = block


def contract(coef_ref, planes, start, acc_init):
    rows_y, cols_z = coef_ref.shape[3:]
    zero = jnp.zeros((GROUP, rows_y, cols_z), jnp.float32)
    acc = [[zero for _ in range(3)] for _ in range(3)]
    for sketch_ref, first in planes:
        for b in range(3):
            own = sketch_ref[b, pl.ds(start, GROUP)]
            for dz in range(3):
                moved = own
                if dz == 0:
                    moved = pltpu.roll(own, 1, 2)
                elif dz == 2:
                    moved = pltpu.roll(own, cols_z - 1, 2)
                for dy in range(3):
                    for a in range(3):
                        acc[dy][a] += coef_ref[first + dy * 3 + dz, a, b][None] * moved
    out = []
    for a in range(3):
        total = acc[1][a] + pltpu.roll(acc[0][a], 1, 1) + pltpu.roll(acc[2][a], rows_y - 1, 1)
        if acc_init is not None:
            total = total + acc_init(a)
        out.append(total)
    return out


def near_kernel(coef_ref, own_ref, pair_ref, part_ref, far_coef_ref, work):
    pair_base, chain_base = side_bases()
    me = lax.axis_index("dom")
    count = lax.axis_size("dom")
    lone = (me == 0) | (me == count - 1)
    rows_y, cols_z = coef_ref.shape[3:]
    keep = iota((rows_y, cols_z), 0) >= jnp.where(lone, rows_y, 0)
    prepare(coef_ref, work, 9, 0, None)
    prepare(coef_ref, work, pair_base, 9, None)
    prepare(coef_ref, far_coef_ref, chain_base, 0, keep)

    def step(i, carry):
        start = i * GROUP
        out = contract(work, [(own_ref, 0), (pair_ref, 9)], start, None)
        for a in range(3):
            part_ref[a, pl.ds(start, GROUP)] = out[a]
        return carry

    lax.fori_loop(0, own_ref.shape[1] // GROUP, step, 0)


def far_kernel(far_coef_ref, chain_ref, part_ref, split_ref, gram_ref, work):
    columns = chain_ref.shape[1]
    rows_y, cols_z = chain_ref.shape[2:]

    def step(i, carry):
        start = i * GROUP
        out = contract(
            far_coef_ref, [(chain_ref, 0)], start, lambda a: part_ref[a, pl.ds(start, GROUP)]
        )
        for a in range(3):
            work[a, pl.ds(start * rows_y, GROUP * rows_y)] = out[a].reshape(GROUP * rows_y, cols_z)
        return carry

    lax.fori_loop(0, columns // GROUP, step, 0)
    total = jnp.zeros((2 * columns, 2 * columns), jnp.float32)
    for a in range(3):
        for y in range(0, rows_y, 2):
            both = []
            for yy in (y, y + 1):
                x = work[a, pl.ds(yy, columns, stride=rows_y)]
                high = x.astype(jnp.bfloat16)
                low = (x - high.astype(jnp.float32)).astype(jnp.bfloat16)
                stack = jnp.concatenate([high, low], axis=0)
                both.append(stack)
            wide = jnp.concatenate(both, axis=1)
            split_ref[(a * rows_y + y) // 2] = wide
            total += lax.dot_general(
                wide, wide, (((1,), (1,)), ((), ())), preferred_element_type=jnp.float32
            )
    rows = total[:columns] + total[columns:]
    gram = rows + pltpu.roll(rows, columns, 1)
    half = columns // 2
    lane = iota((half, 2 * columns), 1)
    gram_ref[...] = jnp.where(lane < columns, gram[:half], gram[half:])


def factor_rows(gram, columns):
    half = columns // 2
    lane = iota((half, 2 * columns), 1)
    sub = iota((half, 2 * columns), 0)
    top = jnp.where(lane < columns, gram, jnp.where(lane - columns == sub, 1.0, 0.0))
    low = jnp.where(
        lane < columns,
        pltpu.roll(gram, columns, 1),
        jnp.where(lane - columns == sub + half, 1.0, 0.0),
    )
    count = columns // 8
    shape = (8, 2 * columns)
    blocks = [top[8 * j : 8 * j + 8] for j in range(count // 2)]
    blocks += [low[8 * j : 8 * j + 8] for j in range(count // 2)]
    sub8 = iota(shape, 0)
    done = []
    for j in range(count):
        panel = [
            [
                jnp.broadcast_to(blocks[r][:, 8 * j + c : 8 * j + c + 1], shape)
                for c in range(8)
            ]
            for r in range(j, count)
        ]
        live = blocks[j:]
        pivots = jnp.ones(shape, jnp.float32)
        for i in range(8):
            row = jnp.broadcast_to(live[0][i : i + 1], shape)
            heads = {
                c: jnp.broadcast_to(panel[0][c][i : i + 1], shape) for c in range(i, 8)
            }
            inverse = 1.0 / heads[i]
            pivots = jnp.where(sub8 == i, heads[i], pivots)
            for r in range(count - j):
                scale = panel[r][i] * inverse
                if r == 0:
                    if i == 7:
                        continue
                    scale = jnp.where(sub8 > i, scale, 0.0)
                for c in range(i + 1, 8):
                    panel[r][c] = panel[r][c] - scale * heads[c]
                live[r] = live[r] - scale * row
        blocks[j + 1 :] = live[1:]
        done.append(live[0] * (1.0 / jnp.sqrt(pivots)))
    return jnp.concatenate(done, axis=0)


def basis_kernel(gram_ref, split_ref, basis_ref, factor_ref, *, scale):
    half, width = gram_ref.shape
    columns = 2 * half
    scaled = factor_rows(gram_ref[...] / scale, columns)
    lane = iota((columns, width), 1)
    sub = iota((columns, width), 0)
    factor_ref[...] = jnp.where(lane >= sub, scaled, 0.0)[:, :columns]
    right = jnp.where(lane >= columns, scaled, 0.0)
    twice = right + pltpu.roll(right, columns, 1)
    high = twice.astype(jnp.bfloat16)
    low = (twice - high.astype(jnp.float32)).astype(jnp.bfloat16)
    left = jnp.concatenate([high, low], axis=0)
    rows_y = basis_ref.shape[1] // columns
    cols_z = basis_ref.shape[2]
    for a in range(3):
        for y in range(0, rows_y, 2):
            wide = jnp.dot(
                left, split_ref[(a * rows_y + y) // 2], preferred_element_type=jnp.float32
            )
            wide = wide[:columns] + wide[columns:]
            for k in range(2):
                basis_ref[a, pl.ds(y + k, columns, stride=rows_y)] = wide[
                    :, k * cols_z : (k + 1) * cols_z
                ]


def vmem(count):
    return [pl.BlockSpec(memory_space=pltpu.VMEM)] * count


def params():
    return pltpu.CompilerParams(vmem_limit_bytes=VMEM_LIMIT)


def sum_over_devices(x):
    count = lax.axis_size("dom")
    bit = 1
    while bit < count:
        if bit == 1 or bit * 2 >= count:
            masks = [bit]
        else:
            masks = [bit, 2 * bit, 3 * bit]
        parts = [
            lax.ppermute(x, "dom", [(i, i ^ m) for i in range(count)]) for m in masks
        ]
        for part in parts:
            x = x + part
        bit *= len(masks) + 1
    return x


def shards(coefficients, sketch):
    count = lax.axis_size("dom")
    coefs = coefficients[0]
    own = sketch[0]
    _, columns, rows_y, cols_z = own.shape
    chain = [(i, (i + 1) % count) for i in range(1, count, 2)]
    chain += [(b, a) for a, b in chain]
    chain_plane = lax.ppermute(own, "dom", chain)
    pair_plane = lax.ppermute(own, "dom", [(i, i ^ 1) for i in range(count)])
    part, far_coefs = pl.pallas_call(
        near_kernel,
        out_shape=(
            jax.ShapeDtypeStruct(own.shape, jnp.float32),
            jax.ShapeDtypeStruct((9, 3, 3, rows_y, cols_z), jnp.float32),
        ),
        in_specs=vmem(3),
        out_specs=tuple(vmem(2)),
        scratch_shapes=[pltpu.VMEM((18, 3, 3, rows_y, cols_z), jnp.float32)],
        compiler_params=params(),
        cost_estimate=pl.CostEstimate(
            flops=2 * 162 * own.size // 3, bytes_accessed=4 * own.size * 5, transcendentals=0
        ),
        name="near",
    )(coefs, own, pair_plane)
    split, gram = pl.pallas_call(
        far_kernel,
        out_shape=(
            jax.ShapeDtypeStruct((3 * rows_y // 2, 2 * columns, 2 * cols_z), jnp.bfloat16),
            jax.ShapeDtypeStruct((columns // 2, 2 * columns), jnp.float32),
        ),
        in_specs=vmem(3),
        out_specs=tuple(vmem(2)),
        scratch_shapes=[pltpu.VMEM((3, columns * rows_y, cols_z), jnp.float32)],
        compiler_params=params(),
        name="far",
    )(far_coefs, chain_plane, part)
    gram = sum_over_devices(gram)
    scale = 3.0 * count * rows_y * cols_z
    basis, factor = pl.pallas_call(
        lambda *refs: basis_kernel(*refs, scale=scale),
        out_shape=(
            jax.ShapeDtypeStruct((3, columns * rows_y, cols_z), jnp.float32),
            jax.ShapeDtypeStruct((columns, columns), jnp.float32),
        ),
        in_specs=vmem(2),
        out_specs=tuple(vmem(2)),
        compiler_params=params(),
        name="basis",
    )(gram, split)
    return basis.reshape(sketch.shape), factor


def solution(mesh):
    placed = (P("dom", None, None, None, None, None), P("dom", None, None, None, None))
    return jax.shard_map(
        shards,
        mesh=mesh,
        in_specs=placed,
        out_specs=(P("dom", None, None, None, None), P()),
        check_vma=False,
    )
```

time: 351 us -> 45.1 us (0.13)
  local copies, waits for them, and re-layouts: 121 us -> 2.34 us
  matrix products: 105 us -> 0 us
  blocking collectives: 49.8 us -> 0 us
  loops' own time: 48.3 us -> 0 us
  other arithmetic: 17.8 us -> 0.02 us
  starting transfers between devices: 3.7 us -> 19.8 us
  waiting for transfers between devices: 0.01 us -> 12.2 us
  Pallas kernels: 0 us -> 9.83 us
    dot_general x130 -> x0, matrix products: 105 us -> none  [the longest x64 93.9 us: row_step(): jnp.dot(upper_row, solved, precision=lax.Precision.HIGHEST, preferred_ele...]
    dynamic_slice x128 -> x0, local copies, waits for them, and re-layouts: 77.3 us -> none  [the longest x64 39.6 us: column_step(): lax.dynamic_index_in_dim(remain, column, 0, keepdims=False)]
    psum x1 -> x0, blocking collectives: 49.8 us -> none  [shards(): gram_total = lax.psum(gram_local, 'dom')]
    another operation x2 -> x0, loops' own time: 48.3 us -> none  [the longest x1 46.3 us: upper_factor(): lower = lax.fori_loop(0, order, column_step, jnp.zeros_like(gram_matrix))]
    mul x93 -> x0, local copies, waits for them, and re-layouts: 20.5 us -> none  [apply_blocks(): coefficients[:, offset_index, :, source][:, :, None]]
    ppermute x2 -> x9, starting transfers between devices: 3.7 us -> 19.8 us  [the longest x7 12.7 us: sum_over_devices(): lax.ppermute(x, 'dom', [(i, i ^ m) for i in range(count)])]
    dynamic_update_slice x128 -> x0, local copies, waits for them, and re-layouts: 15 us -> none  [the longest x64 13.3 us: column_step(): return lax.dynamic_update_index_in_dim(lower, new_column, column, 1)]
    ppermute x2 -> x9, waiting for transfers between devices: 0.01 us -> 12.2 us  [the longest x7 8.43 us: sum_over_devices(): lax.ppermute(x, 'dom', [(i, i ^ m) for i in range(count)])]
  transfers between devices with their start and end apart: 2 -> 9, of which waited for: 0 -> 7; matrix products, arithmetic and copies ran while one was open for 3% -> 0% of each run, Pallas kernels for 0% -> 9%
where the time goes in v1:
time: 45.1 us; the launch traced here: 44.9 us
  starting transfers between devices  19.8 us (44%)
  waiting for transfers between devices  12.2 us (27%)
  Pallas kernels  9.83 us (22%)
  local copies, waits for them, and re-layouts  2.34 us (5%)
  between operations  0.66 us (1%)
    ppermute x7, starting transfers between devices, sum_over_devices(): lax.ppermute(x, 'dom', [(i, i ^ m) for i in range(count)])  12.7 us
    ppermute x7, waiting for transfers between devices, sum_over_devices(): lax.ppermute(x, 'dom', [(i, i ^ m) for i in range(count)])  8.43 us
    ppermute x1, starting transfers between devices, shards(): chain_plane = lax.ppermute(own, 'dom', chain)  6.59 us
    pallas_call x1, Pallas kernels, shards(): pl.pallas_call(near_kernel, out_shape=(jax.ShapeDtypeStruct(own.shape, jn...  3.83 us
    ppermute x1, waiting for transfers between devices, shards(): chain_plane = lax.ppermute(own, 'dom', chain)  3.81 us
    pallas_call x1, Pallas kernels, shards(): pl.pallas_call(lambda *refs: basis_kernel(*refs, scale=scale), out_shape=...  3.06 us
    pallas_call x1, Pallas kernels, shards(): pl.pallas_call(far_kernel, out_shape=(jax.ShapeDtypeStruct((3 * rows_y //...  2.94 us
    unnamed x4, local copies, waits for them, and re-layouts  2.34 us
  transfers between devices with their start and end apart: 9, of which 7 were waited for; matrix products, arithmetic and copies ran while one was open for 0% of the time, Pallas kernels for 9%

profile of v1, /device:TPU:0, one launch (start us, length us, event | category | flops | bytes accessed | tf_op | source)
XLA Modules:
  0.0 44.9 jit_solution(16188432521398999840)
XLA Ops:
  0.6 0.5 %collective-permute-start = (f32[3,64,8,128]{3,2,1,0:T(8,128)}, f32[3,64,8,128]{3,2,1,0:T(8,128)S(1)}, u32[]{:S(2)}, u32[]{:S(2)}) collective-permute-start(f32[3,64,8,128]{3,2,1,0:T(8,128)} %bitcast.4), channel_id=1, source_target_pairs={{0,1},{1,0},{2,3},{3,2},{4,5},{5,4},{6,7},{7,6},{8,9},{9,8},{10,11... | collective-permute-start | bytes 2359304 | tf_op jit(solution)/shard_map/ppermute | solution.py:242
  1.1 6.6 %collective-permute-start.1 = (f32[3,64,8,128]{3,2,1,0:T(8,128)}, f32[3,64,8,128]{3,2,1,0:T(8,128)S(1)}, u32[]{:S(2)}, u32[]{:S(2)}) collective-permute-start(f32[3,64,8,128]{3,2,1,0:T(8,128)} %bitcast.5), channel_id=1, source_target_pairs={{1,2},{3,4},{5,6},{7,8},{9,10},{11,12},{13,14},{15,16},{17,18},{19... | collective-permute-start | bytes 2359304 | tf_op jit(solution)/shard_map/ppermute | solution.py:241
  7.7 0.0 collective-permute-done.pair_ref
  7.7 0.0 copy-start
  7.7 1.2 %copy-done = f32[1,27,3,3,8,128]{5,4,3,2,1,0:T(8,128)S(1)} copy-done((f32[1,27,3,3,8,128]{5,4,3,2,1,0:T(8,128)S(1)}, f32[1,27,3,3,8,128]{5,4,3,2,1,0:T(8,128)}, u32[]{:S(2)}) %copy-start) | copy-done | bytes 995352
  9.0 0.0 copy-start.1
  9.0 1.1 %copy-done.1 = f32[1,3,64,8,128]{4,3,2,1,0:T(8,128)S(1)} copy-done((f32[1,3,64,8,128]{4,3,2,1,0:T(8,128)S(1)}, f32[1,3,64,8,128]{4,3,2,1,0:T(8,128)}, u32[]{:S(2)}) %copy-start.1) | copy-done | bytes 786456
  10.1 3.8 %near.1 = (f32[3,64,8,128]{3,2,1,0:T(8,128)S(1)}, f32[9,3,3,8,128]{4,3,2,1,0:T(8,128)S(1)}) custom-call(f32[27,3,3,8,128]{4,3,2,1,0:T(8,128)S(1)} %bitcast.3, f32[3,64,8,128]{3,2,1,0:T(8,128)S(1)} %bitcast.6, f32[3,64,8,128]{3,2,1,0:T(8,128)S(1)} %collective-permute-done.pair_ref), custom_call_target="tpu_custom_call" | custom-call | flops 21233664 | bytes 3932160 | tf_op jit(solution)/shard_map/near/pallas_call | solution.py:243
  13.9 3.8 %collective-permute-done.1.chain_ref = f32[3,64,8,128]{3,2,1,0:T(8,128)S(1)} collective-permute-done((f32[3,64,8,128]{3,2,1,0:T(8,128)}, f32[3,64,8,128]{3,2,1,0:T(8,128)S(1)}, u32[]{:S(2)}, u32[]{:S(2)}) %collective-permute-start.1) | collective-permute-done | bytes 786464 | tf_op jit(solution)/shard_map/ppermute | solution.py:241
  17.7 2.9 %far.1 = (bf16[12,128,256]{2,1,0:T(8,128)(2,1)S(1)}, f32[32,128]{1,0:T(8,128)S(1)}) custom-call(f32[9,3,3,8,128]{4,3,2,1,0:T(8,128)S(1)} %get-tuple-element.8.far_coef_ref, f32[3,64,8,128]{3,2,1,0:T(8,128)S(1)} %collective-permute-done.1.chain_ref, f32[3,64,8,128]{3,2,1,0:T(8,128)S(1)} %get-tuple-element.9.part_ref), custom_call_target="tpu_custom_call" | custom-call | tf_op jit(solution)/shard_map/far/pallas_call | solution.py:258
  20.7 3.8 %collective-permute-start.2 = (f32[32,128]{1,0:T(8,128)S(1)}, f32[32,128]{1,0:T(8,128)S(1)}, u32[]{:S(2)}, u32[]{:S(2)}) collective-permute-start(f32[32,128]{1,0:T(8,128)S(1)} %get-tuple-element.10), channel_id=1, source_target_pairs={{0,1},{1,0},{2,3},{3,2},{4,5},{5,4},{6,7},{7,6},{8,9},{9,8},{10,11... | collective-permute-start | bytes 49160 | tf_op jit(solution)/shard_map/ppermute | solution.py:226
  24.5 0.8 %collective-permute-done.2 = f32[32,128]{1,0:T(8,128)S(1)} collective-permute-done((f32[32,128]{1,0:T(8,128)S(1)}, f32[32,128]{1,0:T(8,128)S(1)}, u32[]{:S(2)}, u32[]{:S(2)}) %collective-permute-start.2) | collective-permute-done | bytes 16416 | tf_op jit(solution)/shard_map/ppermute | solution.py:226
  25.4 3.1 %collective-permute-start.5 = (f32[32,128]{1,0:T(8,128)S(1)}, f32[32,128]{1,0:T(8,128)S(1)}, u32[]{:S(2)}, u32[]{:S(2)}) collective-permute-start(f32[32,128]{1,0:T(8,128)S(1)} %add.21), channel_id=1, source_target_pairs={{0,6},{1,7},{2,4},{3,5},{4,2},{5,3},{6,0},{7,1},{8,14},{9,15},{10,... | collective-permute-start | bytes 49160 | tf_op jit(solution)/shard_map/ppermute | solution.py:226
  28.4 1.4 %collective-permute-start.4 = (f32[32,128]{1,0:T(8,128)S(1)}, f32[32,128]{1,0:T(8,128)S(1)}, u32[]{:S(2)}, u32[]{:S(2)}) collective-permute-start(f32[32,128]{1,0:T(8,128)S(1)} %add.21), channel_id=1, source_target_pairs={{0,4},{1,5},{2,6},{3,7},{4,0},{5,1},{6,2},{7,3},{8,12},{9,13},{10,... | collective-permute-start | bytes 49160 | tf_op jit(solution)/shard_map/ppermute | solution.py:226
  29.9 0.0 collective-permute-start.3
  29.9 0.3 collective-permute-done.5
  30.1 2.0 %collective-permute-done.4 = f32[32,128]{1,0:T(8,128)S(1)} collective-permute-done((f32[32,128]{1,0:T(8,128)S(1)}, f32[32,128]{1,0:T(8,128)S(1)}, u32[]{:S(2)}, u32[]{:S(2)}) %collective-permute-start.4) | collective-permute-done | bytes 16416 | tf_op jit(solution)/shard_map/ppermute | solution.py:226
  32.2 1.4 %collective-permute-done.3 = f32[32,128]{1,0:T(8,128)S(1)} collective-permute-done((f32[32,128]{1,0:T(8,128)S(1)}, f32[32,128]{1,0:T(8,128)S(1)}, u32[]{:S(2)}, u32[]{:S(2)}) %collective-permute-start.3) | collective-permute-done | bytes 16416 | tf_op jit(solution)/shard_map/ppermute | solution.py:226
  33.6 3.6 %collective-permute-start.8 = (f32[32,128]{1,0:T(8,128)S(1)}, f32[32,128]{1,0:T(8,128)S(1)}, u32[]{:S(2)}, u32[]{:S(2)}) collective-permute-start(f32[32,128]{1,0:T(8,128)S(1)} %add_add_fusion.1), channel_id=1, source_target_pairs={{0,24},{1,25},{2,26},{3,27},{4,28},{5,29},{6,30},{7,31},{8,16},{9,... | collective-permute-start | bytes 49160 | tf_op jit(solution)/shard_map/ppermute | solution.py:226
  37.2 0.0 collective-permute-start.7
  37.2 0.8 %collective-permute-start.6 = (f32[32,128]{1,0:T(8,128)S(1)}, f32[32,128]{1,0:T(8,128)S(1)}, u32[]{:S(2)}, u32[]{:S(2)}) collective-permute-start(f32[32,128]{1,0:T(8,128)S(1)} %add_add_fusion.1), channel_id=1, source_target_pairs={{0,8},{1,9},{2,10},{3,11},{4,12},{5,13},{6,14},{7,15},{8,0},{9,1},... | collective-permute-start | bytes 49160 | tf_op jit(solution)/shard_map/ppermute | solution.py:226
  38.0 1.1 %collective-permute-done.8 = f32[32,128]{1,0:T(8,128)S(1)} collective-permute-done((f32[32,128]{1,0:T(8,128)S(1)}, f32[32,128]{1,0:T(8,128)S(1)}, u32[]{:S(2)}, u32[]{:S(2)}) %collective-permute-start.8) | collective-permute-done | bytes 16416 | tf_op jit(solution)/shard_map/ppermute | solution.py:226
  39.1 2.7 %collective-permute-done.7 = f32[32,128]{1,0:T(8,128)S(1)} collective-permute-done((f32[32,128]{1,0:T(8,128)S(1)}, f32[32,128]{1,0:T(8,128)S(1)}, u32[]{:S(2)}, u32[]{:S(2)}) %collective-permute-start.7) | collective-permute-done | bytes 16416 | tf_op jit(solution)/shard_map/ppermute | solution.py:226
  41.8 0.0 collective-permute-done.6
  41.9 3.1 %basis.1 = (f32[3,512,128]{2,1,0:T(8,128)}, f32[64,64]{1,0:T(8,128)}) custom-call(f32[32,128]{1,0:T(8,128)S(1)} %add_add_fusion.refs_0_, bf16[12,128,256]{2,1,0:T(8,128)(2,1)S(1)} %get-tuple-element.11.refs_1_), custom_call_target="tpu_custom_call" | custom-call | tf_op jit(solution)/shard_map/basis/pallas_call | solution.py:272
  (3 shorter events, 0.0 us)
Async XLA Ops:
  0.6 7.1 %collective-permute-start = (f32[3,64,8,128]{3,2,1,0:T(8,128)}, f32[3,64,8,128]{3,2,1,0:T(8,128)S(1)}, u32[]{:S(2)}, u32[]{:S(2)}) collective-permute-start(f32[3,64,8,128]{3,2,1,0:T(8,128)} %bitcast.4), channel_id=1, source_target_pairs={{0,1},{1,0},{2,3},{3,2},{4,5},{5,4},{6,7},{7,6},{8,9},{9,8},{10,11... | collective-permute-start | bytes 2359304 | tf_op jit(solution)/shard_map/ppermute | solution.py:242
  1.1 16.6 %collective-permute-start.1 = (f32[3,64,8,128]{3,2,1,0:T(8,128)}, f32[3,64,8,128]{3,2,1,0:T(8,128)S(1)}, u32[]{:S(2)}, u32[]{:S(2)}) collective-permute-start(f32[3,64,8,128]{3,2,1,0:T(8,128)} %bitcast.5), channel_id=1, source_target_pairs={{1,2},{3,4},{5,6},{7,8},{9,10},{11,12},{13,14},{15,16},{17,18},{19... | collective-permute-start | bytes 2359304 | tf_op jit(solution)/shard_map/ppermute | solution.py:241
  7.7 1.2 %copy-start = (f32[1,27,3,3,8,128]{5,4,3,2,1,0:T(8,128)S(1)}, f32[1,27,3,3,8,128]{5,4,3,2,1,0:T(8,128)}, u32[]{:S(2)}) copy-start(f32[1,27,3,3,8,128]{5,4,3,2,1,0:T(8,128)} %param.2) | copy-start | bytes 2985988
  9.0 1.1 %copy-start.1 = (f32[1,3,64,8,128]{4,3,2,1,0:T(8,128)S(1)}, f32[1,3,64,8,128]{4,3,2,1,0:T(8,128)}, u32[]{:S(2)}) copy-start(f32[1,3,64,8,128]{4,3,2,1,0:T(8,128)} %param.3) | copy-start | bytes 2359300
  20.7 4.7 %collective-permute-start.2 = (f32[32,128]{1,0:T(8,128)S(1)}, f32[32,128]{1,0:T(8,128)S(1)}, u32[]{:S(2)}, u32[]{:S(2)}) collective-permute-start(f32[32,128]{1,0:T(8,128)S(1)} %get-tuple-element.10), channel_id=1, source_target_pairs={{0,1},{1,0},{2,3},{3,2},{4,5},{5,4},{6,7},{7,6},{8,9},{9,8},{10,11... | collective-permute-start | bytes 49160 | tf_op jit(solution)/shard_map/ppermute | solution.py:226
  25.4 4.8 %collective-permute-start.5 = (f32[32,128]{1,0:T(8,128)S(1)}, f32[32,128]{1,0:T(8,128)S(1)}, u32[]{:S(2)}, u32[]{:S(2)}) collective-permute-start(f32[32,128]{1,0:T(8,128)S(1)} %add.21), channel_id=1, source_target_pairs={{0,6},{1,7},{2,4},{3,5},{4,2},{5,3},{6,0},{7,1},{8,14},{9,15},{10,... | collective-permute-start | bytes 49160 | tf_op jit(solution)/shard_map/ppermute | solution.py:226
  28.4 3.7 %collective-permute-start.4 = (f32[32,128]{1,0:T(8,128)S(1)}, f32[32,128]{1,0:T(8,128)S(1)}, u32[]{:S(2)}, u32[]{:S(2)}) collective-permute-start(f32[32,128]{1,0:T(8,128)S(1)} %add.21), channel_id=1, source_target_pairs={{0,4},{1,5},{2,6},{3,7},{4,0},{5,1},{6,2},{7,3},{8,12},{9,13},{10,... | collective-permute-start | bytes 49160 | tf_op jit(solution)/shard_map/ppermute | solution.py:226
  29.9 3.7 %collective-permute-start.3 = (f32[32,128]{1,0:T(8,128)S(1)}, f32[32,128]{1,0:T(8,128)S(1)}, u32[]{:S(2)}, u32[]{:S(2)}) collective-permute-start(f32[32,128]{1,0:T(8,128)S(1)} %add.21), channel_id=1, source_target_pairs={{0,2},{1,3},{2,0},{3,1},{4,6},{5,7},{6,4},{7,5},{8,10},{9,11},{10,... | collective-permute-start | bytes 49160 | tf_op jit(solution)/shard_map/ppermute | solution.py:226
  33.6 5.5 %collective-permute-start.8 = (f32[32,128]{1,0:T(8,128)S(1)}, f32[32,128]{1,0:T(8,128)S(1)}, u32[]{:S(2)}, u32[]{:S(2)}) collective-permute-start(f32[32,128]{1,0:T(8,128)S(1)} %add_add_fusion.1), channel_id=1, source_target_pairs={{0,24},{1,25},{2,26},{3,27},{4,28},{5,29},{6,30},{7,31},{8,16},{9,... | collective-permute-start | bytes 49160 | tf_op jit(solution)/shard_map/ppermute | solution.py:226
  37.2 4.6 %collective-permute-start.7 = (f32[32,128]{1,0:T(8,128)S(1)}, f32[32,128]{1,0:T(8,128)S(1)}, u32[]{:S(2)}, u32[]{:S(2)}) collective-permute-start(f32[32,128]{1,0:T(8,128)S(1)} %add_add_fusion.1), channel_id=1, source_target_pairs={{0,16},{1,17},{2,18},{3,19},{4,20},{5,21},{6,22},{7,23},{8,24},{9,... | collective-permute-start | bytes 49160 | tf_op jit(solution)/shard_map/ppermute | solution.py:226
  37.2 4.6 %collective-permute-start.6 = (f32[32,128]{1,0:T(8,128)S(1)}, f32[32,128]{1,0:T(8,128)S(1)}, u32[]{:S(2)}, u32[]{:S(2)}) collective-permute-start(f32[32,128]{1,0:T(8,128)S(1)} %add_add_fusion.1), channel_id=1, source_target_pairs={{0,8},{1,9},{2,10},{3,11},{4,12},{5,13},{6,14},{7,15},{8,0},{9,1},... | collective-permute-start | bytes 49160 | tf_op jit(solution)/shard_map/ppermute | solution.py:226

commit v2 on v1

--- a/solution.py
+++ b/solution.py
@@ -1,3 +1,5 @@
+import functools
+
 import jax
 import jax.numpy as jnp
 from jax import lax
@@ -51,27 +53,26 @@
                     out_ref[first + dy * 3 + dz, a, b] = block
 
 
-def contract(coef_ref, planes, start, acc_init):
+def contract(coef_ref, parts, start, initial):
     rows_y, cols_z = coef_ref.shape[3:]
     zero = jnp.zeros((GROUP, rows_y, cols_z), jnp.float32)
     acc = [[zero for _ in range(3)] for _ in range(3)]
-    for sketch_ref, first in planes:
-        for b in range(3):
-            own = sketch_ref[b, pl.ds(start, GROUP)]
-            for dz in range(3):
-                moved = own
-                if dz == 0:
-                    moved = pltpu.roll(own, 1, 2)
-                elif dz == 2:
-                    moved = pltpu.roll(own, cols_z - 1, 2)
-                for dy in range(3):
-                    for a in range(3):
-                        acc[dy][a] += coef_ref[first + dy * 3 + dz, a, b][None] * moved
+    for sketch_ref, slot, b, first in parts:
+        own = sketch_ref[slot, pl.ds(start, GROUP)]
+        for dz in range(3):
+            moved = own
+            if dz == 0:
+                moved = pltpu.roll(own, 1, 2)
+            elif dz == 2:
+                moved = pltpu.roll(own, cols_z - 1, 2)
+            for dy in range(3):
+                for a in range(3):
+                    acc[dy][a] += coef_ref[first + dy * 3 + dz, a, b][None] * moved
     out = []
     for a in range(3):
         total = acc[1][a] + pltpu.roll(acc[0][a], 1, 1) + pltpu.roll(acc[2][a], rows_y - 1, 1)
-        if acc_init is not None:
-            total = total + acc_init(a)
+        if initial is not None:
+            total = total + initial[a, pl.ds(start, GROUP)]
         out.append(total)
     return out
 
@@ -86,10 +87,11 @@
     prepare(coef_ref, work, 9, 0, None)
     prepare(coef_ref, work, pair_base, 9, None)
     prepare(coef_ref, far_coef_ref, chain_base, 0, keep)
+    parts = [(own_ref, b, b, 0) for b in range(3)] + [(pair_ref, b, b, 9) for b in range(3)]
 
     def step(i, carry):
         start = i * GROUP
-        out = contract(work, [(own_ref, 0), (pair_ref, 9)], start, None)
+        out = contract(work, parts, start, None)
         for a in range(3):
             part_ref[a, pl.ds(start, GROUP)] = out[a]
         return carry
@@ -97,17 +99,46 @@
     lax.fori_loop(0, own_ref.shape[1] // GROUP, step, 0)
 
 
-def far_kernel(far_coef_ref, chain_ref, part_ref, split_ref, gram_ref, work):
+def middle_kernel(far_coef_ref, chain_ref, part_ref, out_ref, *, component):
+    def step(i, carry):
+        start = i * GROUP
+        out = contract(far_coef_ref, [(chain_ref, 0, component, 0)], start, part_ref)
+        for a in range(3):
+            out_ref[a, pl.ds(start, GROUP)] = out[a]
+        return carry
+
+    lax.fori_loop(0, chain_ref.shape[1] // GROUP, step, 0)
+
+
+def pack(gram, half, columns):
+    quarter = columns // 4
+    width = 2 * columns
+    lane = iota((quarter, width), 1) % columns
+    sub = iota((quarter, width), 0)
+    base = half * 2 * quarter
+    first = pltpu.roll(gram[base : base + quarter], (width - base) % width, 1)
+    second = pltpu.roll(gram[base + quarter : base + 2 * quarter], width - base - quarter, 1)
+    cross = gram[half * quarter : (half + 1) * quarter]
+    packed = jnp.where(
+        (lane < quarter) & (lane < sub), second, jnp.where(lane < 2 * quarter, first, cross)
+    )
+    last = jnp.sum(jnp.where(lane == sub, second, 0.0), axis=0, keepdims=True)
+    wide = iota((8, width), 1)
+    return [jnp.where(wide < columns, packed[:8], packed[8:]), last]
+
+
+def last_kernel(
+    far_coef_ref, chain_ref, part_ref, split_ref, mine_ref, twin_ref, work, *, component
+):
     columns = chain_ref.shape[1]
     rows_y, cols_z = chain_ref.shape[2:]
 
     def step(i, carry):
         start = i * GROUP
-        out = contract(
-            far_coef_ref, [(chain_ref, 0)], start, lambda a: part_ref[a, pl.ds(start, GROUP)]
-        )
+        out = contract(far_coef_ref, [(chain_ref, 0, component, 0)], start, part_ref)
         for a in range(3):
-            work[a, pl.ds(start * rows_y, GROUP * rows_y)] = out[a].reshape(GROUP * rows_y, cols_z)
+            for k in range(GROUP):
+                work[a, pl.ds(start + k, rows_y, stride=columns)] = out[a][k]
         return carry
 
     lax.fori_loop(0, columns // GROUP, step, 0)
@@ -116,11 +147,10 @@
         for y in range(0, rows_y, 2):
             both = []
             for yy in (y, y + 1):
-                x = work[a, pl.ds(yy, columns, stride=rows_y)]
+                x = work[a, pl.ds(yy * columns, columns)]
                 high = x.astype(jnp.bfloat16)
                 low = (x - high.astype(jnp.float32)).astype(jnp.bfloat16)
-                stack = jnp.concatenate([high, low], axis=0)
-                both.append(stack)
+                both.append(jnp.concatenate([high, low], axis=0))
             wide = jnp.concatenate(both, axis=1)
             split_ref[(a * rows_y + y) // 2] = wide
             total += lax.dot_general(
@@ -128,25 +158,64 @@
             )
     rows = total[:columns] + total[columns:]
     gram = rows + pltpu.roll(rows, columns, 1)
-    half = columns // 2
-    lane = iota((half, 2 * columns), 1)
-    gram_ref[...] = jnp.where(lane < columns, gram[:half], gram[half:])
+    odd = lax.axis_index("dom") % 2 == 1
+    halves = [pack(gram, h, columns) for h in range(2)]
+    for ref, flip in ((mine_ref, False), (twin_ref, True)):
+        low, high = halves[::-1] if flip else halves
+        body = jnp.where(odd, high[0], low[0])
+        for r in range(8):
+            ref[:, r * 2 * columns : (r + 1) * 2 * columns] = body[r : r + 1]
+        ref[:, 16 * columns :] = jnp.where(odd, high[1], low[1])
+
+
+def unpack(parts_ref, columns):
+    width = 2 * columns
+    quarter = columns // 4
+    sub8 = iota((8, width), 0)
+    rows = []
+    for r in range(9):
+        x = parts_ref[:, 0, r * width : (r + 1) * width]
+        x = jnp.sum(x.reshape(x.shape[0] // 8, 8, width), axis=0)
+        x = x + pltpu.roll(x, 2, 0)
+        rows.append(x + pltpu.roll(x, 4, 0))
+    lane = iota((quarter, width), 1)
+    sub = iota((quarter, width), 0)
+    out = []
+    for half in range(2):
+        body = jnp.zeros((8, width), jnp.float32)
+        for r in range(8):
+            body = jnp.where(
+                sub8 == r, jnp.broadcast_to(rows[r][half : half + 1], (8, width)), body
+            )
+        packed = jnp.concatenate([body, pltpu.roll(body, columns, 1)], axis=0)
+        base = half * 2 * quarter
+        upper = jnp.where(lane >= sub, packed, 0.0)
+        upper = jnp.where(lane < 2 * quarter, upper, 0.0)
+        lower = jnp.where(lane < sub, packed, 0.0)
+        diag = jnp.broadcast_to(rows[8][half : half + 1], (quarter, width))
+        lower = jnp.where(lane == sub, diag, lower)
+        lower = jnp.where(lane < quarter, lower, 0.0)
+        cross = jnp.where((lane >= 2 * quarter) & (lane < columns), packed, 0.0)
+        if base:
+            upper = pltpu.roll(upper, base, 1)
+        out.append((upper, pltpu.roll(lower, base + quarter, 1), cross))
+    once = jnp.concatenate(
+        [out[0][0] + out[0][2], out[0][1] + out[1][2], out[1][0], out[1][1]], axis=0
+    )
+    lane = iota((columns, width), 1)
+    sub = iota((columns, width), 0)
+    square = jnp.concatenate([once, jnp.zeros_like(once)], axis=0)
+    mirror = jnp.transpose(square)[:columns]
+    return once + jnp.where(lane == sub, 0.0, mirror)
 
 
 def factor_rows(gram, columns):
-    half = columns // 2
-    lane = iota((half, 2 * columns), 1)
-    sub = iota((half, 2 * columns), 0)
-    top = jnp.where(lane < columns, gram, jnp.where(lane - columns == sub, 1.0, 0.0))
-    low = jnp.where(
-        lane < columns,
-        pltpu.roll(gram, columns, 1),
-        jnp.where(lane - columns == sub + half, 1.0, 0.0),
-    )
+    lane = iota(gram.shape, 1)
+    sub = iota(gram.shape, 0)
+    both = jnp.where(lane - columns == sub, 1.0, gram)
     count = columns // 8
     shape = (8, 2 * columns)
-    blocks = [top[8 * j : 8 * j + 8] for j in range(count // 2)]
-    blocks += [low[8 * j : 8 * j + 8] for j in range(count // 2)]
+    blocks = [both[8 * j : 8 * j + 8] for j in range(count)]
     sub8 = iota(shape, 0)
     done = []
     for j in range(count):
@@ -180,10 +249,10 @@
     return jnp.concatenate(done, axis=0)
 
 
-def basis_kernel(gram_ref, split_ref, basis_ref, factor_ref, *, scale):
-    half, width = gram_ref.shape
-    columns = 2 * half
-    scaled = factor_rows(gram_ref[...] / scale, columns)
+def basis_kernel(parts_ref, split_ref, basis_ref, factor_ref, *, scale):
+    columns = factor_ref.shape[0]
+    width = 2 * columns
+    scaled = factor_rows(unpack(parts_ref, columns) / scale, columns)
     lane = iota((columns, width), 1)
     sub = iota((columns, width), 0)
     factor_ref[...] = jnp.where(lane >= sub, scaled, 0.0)[:, :columns]
@@ -214,23 +283,6 @@
     return pltpu.CompilerParams(vmem_limit_bytes=VMEM_LIMIT)
 
 
-def sum_over_devices(x):
-    count = lax.axis_size("dom")
-    bit = 1
-    while bit < count:
-        if bit == 1 or bit * 2 >= count:
-            masks = [bit]
-        else:
-            masks = [bit, 2 * bit, 3 * bit]
-        parts = [
-            lax.ppermute(x, "dom", [(i, i ^ m) for i in range(count)]) for m in masks
-        ]
-        for part in parts:
-            x = x + part
-        bit *= len(masks) + 1
-    return x
-
-
 def shards(coefficients, sketch):
     count = lax.axis_size("dom")
     coefs = coefficients[0]
@@ -238,8 +290,9 @@
     _, columns, rows_y, cols_z = own.shape
     chain = [(i, (i + 1) % count) for i in range(1, count, 2)]
     chain += [(b, a) for a, b in chain]
-    chain_plane = lax.ppermute(own, "dom", chain)
-    pair_plane = lax.ppermute(own, "dom", [(i, i ^ 1) for i in range(count)])
+    faces = [lax.ppermute(own[b : b + 1], "dom", chain) for b in range(3)]
+    pairs = [(i, i ^ 1) for i in range(count)]
+    pair_plane = lax.ppermute(own, "dom", pairs)
     part, far_coefs = pl.pallas_call(
         near_kernel,
         out_shape=(
@@ -255,22 +308,34 @@
         ),
         name="near",
     )(coefs, own, pair_plane)
-    split, gram = pl.pallas_call(
-        far_kernel,
+    for b in range(2):
+        part = pl.pallas_call(
+            functools.partial(middle_kernel, component=b),
+            out_shape=jax.ShapeDtypeStruct(own.shape, jnp.float32),
+            in_specs=vmem(3),
+            out_specs=vmem(1)[0],
+            compiler_params=params(),
+            name="middle",
+        )(far_coefs, faces[b], part)
+    packed = jax.ShapeDtypeStruct((1, 18 * columns), jnp.float32)
+    split, mine, twin = pl.pallas_call(
+        functools.partial(last_kernel, component=2),
         out_shape=(
             jax.ShapeDtypeStruct((3 * rows_y // 2, 2 * columns, 2 * cols_z), jnp.bfloat16),
-            jax.ShapeDtypeStruct((columns // 2, 2 * columns), jnp.float32),
+            packed,
+            packed,
         ),
         in_specs=vmem(3),
-        out_specs=tuple(vmem(2)),
+        out_specs=tuple(vmem(3)),
         scratch_shapes=[pltpu.VMEM((3, columns * rows_y, cols_z), jnp.float32)],
         compiler_params=params(),
-        name="far",
-    )(far_coefs, chain_plane, part)
-    gram = sum_over_devices(gram)
+        name="last",
+    )(far_coefs, faces[2], part)
+    mine = mine + lax.ppermute(twin, "dom", pairs)
+    parts = lax.all_to_all(jnp.broadcast_to(mine, (count,) + mine.shape), "dom", 0, 0)
     scale = 3.0 * count * rows_y * cols_z
     basis, factor = pl.pallas_call(
-        lambda *refs: basis_kernel(*refs, scale=scale),
+        functools.partial(basis_kernel, scale=scale),
         out_shape=(
             jax.ShapeDtypeStruct((3, columns * rows_y, cols_z), jnp.float32),
             jax.ShapeDtypeStruct((columns, columns), jnp.float32),
@@ -279,7 +344,7 @@
         out_specs=tuple(vmem(2)),
         compiler_params=params(),
         name="basis",
-    )(gram, split)
+    )(parts, split)
     return basis.reshape(sketch.shape), factor
 
 

time: 45.1 us -> 44.4 us (0.984)
  blocking collectives: 0 us -> 14.4 us
  waiting for transfers between devices: 12.2 us -> 1.16 us
  starting transfers between devices: 19.8 us -> 12.6 us
  Pallas kernels: 9.83 us -> 12.9 us
    all_to_all x0 -> x1, blocking collectives: none -> 14.4 us  [shards(): lax.all_to_all(jnp.broadcast_to(mine, (count,) + mine.shape), 'dom', 0, 0)]
    ppermute x9 -> x5, waiting for transfers between devices: 12.2 us -> 1.16 us  [the longest x1 1.15 us: shards(): mine = mine + lax.ppermute(twin, 'dom', pairs)]
    ppermute x9 -> x5, starting transfers between devices: 19.8 us -> 12.6 us  [the longest x3 12 us: shards(): faces = [lax.ppermute(own[b:b + 1], 'dom', chain) for b in range(3)]]
    pallas_call x2 -> x4, Pallas kernels: 6 us -> 9.02 us  [the longest x1 3.31 us: shards(): pl.pallas_call(functools.partial(basis_kernel, scale=scale), out_shape=(j...]
    slice x0 -> x1, local copies, waits for them, and re-layouts: none -> 1.16 us  [shards(): faces = [lax.ppermute(own[b:b + 1], 'dom', chain) for b in range(3)]]
    unnamed x4, local copies, waits for them, and re-layouts: 2.34 us -> 1.21 us
  transfers between devices with their start and end apart: 9 -> 5, of which waited for: 7 -> 1; matrix products, arithmetic and copies ran while one was open for 0% -> 3% of each run, Pallas kernels for 9% -> 16%
where the time goes in v2:
time: 44.4 us; the launch traced here: 44.2 us
  blocking collectives  14.4 us (32%)
  Pallas kernels  12.9 us (29%)
  starting transfers between devices  12.6 us (28%)
  local copies, waits for them, and re-layouts  2.45 us (6%)
  waiting for transfers between devices  1.16 us (3%)
  between operations  0.71 us (2%)
    all_to_all x1, blocking collectives, shards(): lax.all_to_all(jnp.broadcast_to(mine, (count,) + mine.shape), 'dom', 0, 0)  14.4 us
    ppermute x3, starting transfers between devices, shards(): faces = [lax.ppermute(own[b:b + 1], 'dom', chain) for b in range(3)]  12 us
    pallas_call x1, Pallas kernels, shards(): pl.pallas_call(near_kernel, out_shape=(jax.ShapeDtypeStruct(own.shape, jn...  3.86 us
    pallas_call x1, Pallas kernels, shards(): pl.pallas_call(functools.partial(basis_kernel, scale=scale), out_shape=(j...  3.31 us
    pallas_call x2, Pallas kernels, shards(): pl.pallas_call(functools.partial(middle_kernel, component=b), out_shape=j...  3.2 us
    pallas_call x1, Pallas kernels, shards(): pl.pallas_call(functools.partial(last_kernel, component=2), out_shape=(ja...  2.52 us
    unnamed x4, local copies, waits for them, and re-layouts  1.21 us
    slice x1, local copies, waits for them, and re-layouts, shards(): faces = [lax.ppermute(own[b:b + 1], 'dom', chain) for b in range(3)]  1.16 us
  transfers between devices with their start and end apart: 5, of which 1 were waited for; matrix products, arithmetic and copies ran while one was open for 3% of the time, Pallas kernels for 16%

profile of v2, /device:TPU:0, one launch (start us, length us, event | category | flops | bytes accessed | tf_op | source)
XLA Modules:
  0.0 44.2 jit_solution(5272194557977134685)
XLA Ops:
  0.6 0.0 copy-start
  0.6 0.5 %collective-permute-start = (f32[3,64,8,128]{3,2,1,0:T(8,128)}, f32[3,64,8,128]{3,2,1,0:T(8,128)S(1)}, u32[]{:S(2)}, u32[]{:S(2)}) collective-permute-start(f32[3,64,8,128]{3,2,1,0:T(8,128)} %bitcast.9), channel_id=1, source_target_pairs={{0,1},{1,0},{2,3},{3,2},{4,5},{5,4},{6,7},{7,6},{8,9},{9,8},{10,11... | collective-permute-start | bytes 2359304 | tf_op jit(solution)/shard_map/ppermute | solution.py:295
  1.2 1.2 %slice_bitcast_fusion = (f32[1,64,8,128]{3,2,1,0:T(8,128)S(1)}, f32[1,64,8,128]{3,2,1,0:T(8,128)S(1)}, f32[1,64,8,128]{3,2,1,0:T(8,128)S(1)}) fusion(f32[1,3,64,8,128]{4,3,2,1,0:T(8,128)} %param.3), kind=kLoop, calls=%fused_computation | loop fusion | bytes 1572864 | tf_op jit(solution)/shard_map/slice | solution.py:293
  2.3 6.7 %collective-permute-start.3 = (f32[1,64,8,128]{3,2,1,0:T(8,128)S(1)}, f32[1,64,8,128]{3,2,1,0:T(8,128)S(1)}, u32[]{:S(2)}, u32[]{:S(2)}) collective-permute-start(f32[1,64,8,128]{3,2,1,0:T(8,128)S(1)} %get-tuple-element.16), channel_id=1, source_target_pairs={{1,2},{3,4},{5,6},{7,8},{9,10},{11,12},{13,14},{15,16},{17,18},{19... | collective-permute-start | bytes 786440 | tf_op jit(solution)/shard_map/ppermute | solution.py:293
  9.0 0.1 collective-permute-start.2
  9.1 5.3 %collective-permute-start.1 = (f32[1,64,8,128]{3,2,1,0:T(8,128)S(1)}, f32[1,64,8,128]{3,2,1,0:T(8,128)S(1)}, u32[]{:S(2)}, u32[]{:S(2)}) collective-permute-start(f32[1,64,8,128]{3,2,1,0:T(8,128)S(1)} %get-tuple-element.17), channel_id=1, source_target_pairs={{1,2},{3,4},{5,6},{7,8},{9,10},{11,12},{13,14},{15,16},{17,18},{19... | collective-permute-start | bytes 786440 | tf_op jit(solution)/shard_map/ppermute | solution.py:293
  14.3 0.0 collective-permute-done.pair_ref
  14.3 0.0 copy-done
  14.3 0.0 copy-start.1
  14.3 1.2 %copy-done.1 = f32[1,27,3,3,8,128]{5,4,3,2,1,0:T(8,128)S(1)} copy-done((f32[1,27,3,3,8,128]{5,4,3,2,1,0:T(8,128)S(1)}, f32[1,27,3,3,8,128]{5,4,3,2,1,0:T(8,128)}, u32[]{:S(2)}) %copy-start.1) | copy-done | bytes 995352
  15.5 3.9 %near.1 = (f32[3,64,8,128]{3,2,1,0:T(8,128)S(1)}, f32[9,3,3,8,128]{4,3,2,1,0:T(8,128)S(1)}) custom-call(f32[27,3,3,8,128]{4,3,2,1,0:T(8,128)S(1)} %bitcast.11, f32[3,64,8,128]{3,2,1,0:T(8,128)S(1)} %bitcast.10, f32[3,64,8,128]{3,2,1,0:T(8,128)S(1)} %collective-permute-done.pair_ref), custom_call_target="tpu_custom_call" | custom-call | flops 21233664 | bytes 3932160 | tf_op jit(solution)/shard_map/near/pallas_call | solution.py:296
  19.4 0.0 collective-permute-done.3.chain_ref
  19.4 1.6 %middle.2.part_ref = f32[3,64,8,128]{3,2,1,0:T(8,128)S(1)} custom-call(f32[9,3,3,8,128]{4,3,2,1,0:T(8,128)S(1)} %get-tuple-element.9.far_coef_ref, f32[1,64,8,128]{3,2,1,0:T(8,128)S(1)} %collective-permute-done.3.chain_ref, f32[3,64,8,128]{3,2,1,0:T(8,128)S(1)} %get-tuple-element.10.part_ref), custom_call_target="tpu_custom_call" | custom-call | tf_op jit(solution)/shard_map/middle/pallas_call | solution.py:312
  21.0 0.0 collective-permute-done.2.chain_ref
  21.0 1.6 %middle.3.part_ref = f32[3,64,8,128]{3,2,1,0:T(8,128)S(1)} custom-call(f32[9,3,3,8,128]{4,3,2,1,0:T(8,128)S(1)} %get-tuple-element.9.far_coef_ref, f32[1,64,8,128]{3,2,1,0:T(8,128)S(1)} %collective-permute-done.2.chain_ref, f32[3,64,8,128]{3,2,1,0:T(8,128)S(1)} %middle.2.part_ref), custom_call_target="tpu_custom_call" | custom-call | tf_op jit(solution)/shard_map/middle/pallas_call | solution.py:312
  22.6 0.0 collective-permute-done.1.chain_ref
  22.6 2.5 %last.1 = (bf16[12,128,256]{2,1,0:T(8,128)(2,1)S(1)}, f32[1,1152]{1,0:T(1,128)S(1)}, f32[1,1152]{1,0:T(1,128)S(1)}) custom-call(f32[9,3,3,8,128]{4,3,2,1,0:T(8,128)S(1)} %get-tuple-element.9.far_coef_ref, f32[1,64,8,128]{3,2,1,0:T(8,128)S(1)} %collective-permute-done.1.chain_ref, f32[3,64,8,128]{3,2,1,0:T(8,128)S(1)} %middle.3.part_ref), custom_call_target="tpu_custom_call" | custom-call | tf_op jit(solution)/shard_map/last/pallas_call | solution.py:321
  25.2 0.1 collective-permute-start.4
  25.2 1.2 %collective-permute-done.4 = f32[1,1152]{1,0:T(1,128)S(1)} collective-permute-done((f32[1,1152]{1,0:T(1,128)S(1)}, f32[1,1152]{1,0:T(1,128)S(1)}, u32[]{:S(2)}, u32[]{:S(2)}) %collective-permute-start.4) | collective-permute-done | bytes 4640 | tf_op jit(solution)/shard_map/ppermute | solution.py:334
  26.4 0.1 broadcast_in_dim.3
  26.5 14.4 %all_to_all.5.parts_ref = f32[32,1,1152]{2,1,0:T(1,128)S(1)} all-to-all(f32[32,1,1152]{2,1,0:T(1,128)S(1)} %broadcast_in_dim.3), channel_id=1, replica_groups=mesh['dom'=32] {'dom'}, dimensions={0} | all-to-all | bytes 294912 | tf_op jit(solution)/shard_map/all_to_all | solution.py:335
  40.9 3.3 %basis.1 = (f32[3,512,128]{2,1,0:T(8,128)}, f32[64,64]{1,0:T(8,128)}) custom-call(f32[32,1,1152]{2,1,0:T(1,128)S(1)} %all_to_all.5.parts_ref, bf16[12,128,256]{2,1,0:T(8,128)(2,1)S(1)} %get-tuple-element.13.split_ref), custom_call_target="tpu_custom_call" | custom-call | tf_op jit(solution)/shard_map/basis/pallas_call | solution.py:337
  (1 shorter events, 0.0 us)
Async XLA Ops:
  0.6 13.7 %copy-start = (f32[1,3,64,8,128]{4,3,2,1,0:T(8,128)S(1)}, f32[1,3,64,8,128]{4,3,2,1,0:T(8,128)}, u32[]{:S(2)}) copy-start(f32[1,3,64,8,128]{4,3,2,1,0:T(8,128)} %param.3) | copy-start | bytes 2359300
  0.6 13.7 %collective-permute-start = (f32[3,64,8,128]{3,2,1,0:T(8,128)}, f32[3,64,8,128]{3,2,1,0:T(8,128)S(1)}, u32[]{:S(2)}, u32[]{:S(2)}) collective-permute-start(f32[3,64,8,128]{3,2,1,0:T(8,128)} %bitcast.9), channel_id=1, source_target_pairs={{0,1},{1,0},{2,3},{3,2},{4,5},{5,4},{6,7},{7,6},{8,9},{9,8},{10,11... | collective-permute-start | bytes 2359304 | tf_op jit(solution)/shard_map/ppermute | solution.py:295
  2.3 17.1 %collective-permute-start.3 = (f32[1,64,8,128]{3,2,1,0:T(8,128)S(1)}, f32[1,64,8,128]{3,2,1,0:T(8,128)S(1)}, u32[]{:S(2)}, u32[]{:S(2)}) collective-permute-start(f32[1,64,8,128]{3,2,1,0:T(8,128)S(1)} %get-tuple-element.16), channel_id=1, source_target_pairs={{1,2},{3,4},{5,6},{7,8},{9,10},{11,12},{13,14},{15,16},{17,18},{19... | collective-permute-start | bytes 786440 | tf_op jit(solution)/shard_map/ppermute | solution.py:293
  9.0 12.0 %collective-permute-start.2 = (f32[1,64,8,128]{3,2,1,0:T(8,128)S(1)}, f32[1,64,8,128]{3,2,1,0:T(8,128)S(1)}, u32[]{:S(2)}, u32[]{:S(2)}) collective-permute-start(f32[1,64,8,128]{3,2,1,0:T(8,128)S(1)} %get-tuple-element.18), channel_id=1, source_target_pairs={{1,2},{3,4},{5,6},{7,8},{9,10},{11,12},{13,14},{15,16},{17,18},{19... | collective-permute-start | bytes 786440 | tf_op jit(solution)/shard_map/ppermute | solution.py:293
  9.1 13.6 %collective-permute-start.1 = (f32[1,64,8,128]{3,2,1,0:T(8,128)S(1)}, f32[1,64,8,128]{3,2,1,0:T(8,128)S(1)}, u32[]{:S(2)}, u32[]{:S(2)}) collective-permute-start(f32[1,64,8,128]{3,2,1,0:T(8,128)S(1)} %get-tuple-element.17), channel_id=1, source_target_pairs={{1,2},{3,4},{5,6},{7,8},{9,10},{11,12},{13,14},{15,16},{17,18},{19... | collective-permute-start | bytes 786440 | tf_op jit(solution)/shard_map/ppermute | solution.py:293
  14.3 1.2 %copy-start.1 = (f32[1,27,3,3,8,128]{5,4,3,2,1,0:T(8,128)S(1)}, f32[1,27,3,3,8,128]{5,4,3,2,1,0:T(8,128)}, u32[]{:S(2)}) copy-start(f32[1,27,3,3,8,128]{5,4,3,2,1,0:T(8,128)} %param.2) | copy-start | bytes 2985988
  25.2 1.2 %collective-permute-start.4 = (f32[1,1152]{1,0:T(1,128)S(1)}, f32[1,1152]{1,0:T(1,128)S(1)}, u32[]{:S(2)}, u32[]{:S(2)}) collective-permute-start(f32[1,1152]{1,0:T(1,128)S(1)} %get-tuple-element.12), channel_id=1, source_target_pairs={{0,1},{1,0},{2,3},{3,2},{4,5},{5,4},{6,7},{7,6},{8,9},{9,8},{10,11... | collective-permute-start | bytes 13832 | tf_op jit(solution)/shard_map/ppermute | solution.py:334

commit v3 on v2

--- a/solution.py
+++ b/solution.py
@@ -8,6 +8,7 @@
 from jax.sharding import PartitionSpec as P
 
 GROUP = 4
+UNROLL = 4
 VMEM_LIMIT = 48 * 1024 * 1024
 
 
@@ -96,18 +97,7 @@
             part_ref[a, pl.ds(start, GROUP)] = out[a]
         return carry
 
-    lax.fori_loop(0, own_ref.shape[1] // GROUP, step, 0)
-
-
-def middle_kernel(far_coef_ref, chain_ref, part_ref, out_ref, *, component):
-    def step(i, carry):
-        start = i * GROUP
-        out = contract(far_coef_ref, [(chain_ref, 0, component, 0)], start, part_ref)
-        for a in range(3):
-            out_ref[a, pl.ds(start, GROUP)] = out[a]
-        return carry
-
-    lax.fori_loop(0, chain_ref.shape[1] // GROUP, step, 0)
+    lax.fori_loop(0, own_ref.shape[1] // GROUP, step, 0, unroll=UNROLL)
 
 
 def pack(gram, half, columns):
@@ -127,27 +117,27 @@
     return [jnp.where(wide < columns, packed[:8], packed[8:]), last]
 
 
-def last_kernel(
-    far_coef_ref, chain_ref, part_ref, split_ref, mine_ref, twin_ref, work, *, component
-):
+def far_kernel(far_coef_ref, chain_ref, part_ref, split_ref, mine_ref, twin_ref, work):
     columns = chain_ref.shape[1]
     rows_y, cols_z = chain_ref.shape[2:]
+    parts = [(chain_ref, b, b, 0) for b in range(3)]
 
     def step(i, carry):
         start = i * GROUP
-        out = contract(far_coef_ref, [(chain_ref, 0, component, 0)], start, part_ref)
+        out = contract(far_coef_ref, parts, start, part_ref)
         for a in range(3):
-            for k in range(GROUP):
-                work[a, pl.ds(start + k, rows_y, stride=columns)] = out[a][k]
+            work[a, pl.ds(start * rows_y, GROUP * rows_y)] = out[a].reshape(
+                GROUP * rows_y, cols_z
+            )
         return carry
 
-    lax.fori_loop(0, columns // GROUP, step, 0)
+    lax.fori_loop(0, columns // GROUP, step, 0, unroll=UNROLL)
     total = jnp.zeros((2 * columns, 2 * columns), jnp.float32)
     for a in range(3):
         for y in range(0, rows_y, 2):
             both = []
             for yy in (y, y + 1):
-                x = work[a, pl.ds(yy * columns, columns)]
+                x = work[a, pl.ds(yy, columns, stride=rows_y)]
                 high = x.astype(jnp.bfloat16)
                 low = (x - high.astype(jnp.float32)).astype(jnp.bfloat16)
                 both.append(jnp.concatenate([high, low], axis=0))
@@ -217,35 +207,45 @@
     shape = (8, 2 * columns)
     blocks = [both[8 * j : 8 * j + 8] for j in range(count)]
     sub8 = iota(shape, 0)
+    def spread(block, column):
+        return jnp.broadcast_to(block[:, column : column + 1], shape)
+
+    def repeat(block, row):
+        return jnp.broadcast_to(block[row : row + 1], shape)
+
     done = []
+    ahead = [spread(blocks[0], c) for c in range(8)]
     for j in range(count):
-        panel = [
-            [
-                jnp.broadcast_to(blocks[r][:, 8 * j + c : 8 * j + c + 1], shape)
-                for c in range(8)
-            ]
-            for r in range(j, count)
-        ]
-        live = blocks[j:]
-        pivots = jnp.ones(shape, jnp.float32)
+        own = ahead
+        mine = blocks[j]
+        rest = range(j + 1, count)
+        if j + 1 < count:
+            ahead = [spread(blocks[j + 1], 8 * (j + 1) + c) for c in range(8)]
+        panel = {r: [spread(blocks[r], 8 * j + c) for c in range(8)] for r in rest}
+        pivots = None
         for i in range(8):
-            row = jnp.broadcast_to(live[0][i : i + 1], shape)
-            heads = {
-                c: jnp.broadcast_to(panel[0][c][i : i + 1], shape) for c in range(i, 8)
-            }
+            heads = {c: repeat(own[c], i) for c in range(i, 8)}
+            row = repeat(mine, i)
             inverse = 1.0 / heads[i]
-            pivots = jnp.where(sub8 == i, heads[i], pivots)
-            for r in range(count - j):
+            pivots = heads[i] if i == 0 else jnp.where(sub8 == i, heads[i], pivots)
+            if i < 7:
+                scale = jnp.where(sub8 > i, own[i] * inverse, 0.0)
+                for c in range(i + 1, 8):
+                    if c == i + 1:
+                        product = jnp.where(sub8 > i, own[i] * heads[c], 0.0)
+                        own[c] = own[c] - product * inverse
+                    else:
+                        own[c] = own[c] - scale * heads[c]
+                mine = mine - scale * row
+            for r in rest:
                 scale = panel[r][i] * inverse
-                if r == 0:
-                    if i == 7:
-                        continue
-                    scale = jnp.where(sub8 > i, scale, 0.0)
+                if r == j + 1:
+                    for c in range(8):
+                        ahead[c] = ahead[c] - scale * repeat(panel[r][i], c)
                 for c in range(i + 1, 8):
                     panel[r][c] = panel[r][c] - scale * heads[c]
-                live[r] = live[r] - scale * row
-        blocks[j + 1 :] = live[1:]
-        done.append(live[0] * (1.0 / jnp.sqrt(pivots)))
+                blocks[r] = blocks[r] - scale * row
+        done.append(mine * (1.0 / jnp.sqrt(pivots)))
     return jnp.concatenate(done, axis=0)
 
 
@@ -290,7 +290,7 @@
     _, columns, rows_y, cols_z = own.shape
     chain = [(i, (i + 1) % count) for i in range(1, count, 2)]
     chain += [(b, a) for a, b in chain]
-    faces = [lax.ppermute(own[b : b + 1], "dom", chain) for b in range(3)]
+    chain_plane = lax.ppermute(own, "dom", chain)
     pairs = [(i, i ^ 1) for i in range(count)]
     pair_plane = lax.ppermute(own, "dom", pairs)
     part, far_coefs = pl.pallas_call(
@@ -308,18 +308,9 @@
         ),
         name="near",
     )(coefs, own, pair_plane)
-    for b in range(2):
-        part = pl.pallas_call(
-            functools.partial(middle_kernel, component=b),
-            out_shape=jax.ShapeDtypeStruct(own.shape, jnp.float32),
-            in_specs=vmem(3),
-            out_specs=vmem(1)[0],
-            compiler_params=params(),
-            name="middle",
-        )(far_coefs, faces[b], part)
     packed = jax.ShapeDtypeStruct((1, 18 * columns), jnp.float32)
     split, mine, twin = pl.pallas_call(
-        functools.partial(last_kernel, component=2),
+        far_kernel,
         out_shape=(
             jax.ShapeDtypeStruct((3 * rows_y // 2, 2 * columns, 2 * cols_z), jnp.bfloat16),
             packed,
@@ -329,8 +320,8 @@
         out_specs=tuple(vmem(3)),
         scratch_shapes=[pltpu.VMEM((3, columns * rows_y, cols_z), jnp.float32)],
         compiler_params=params(),
-        name="last",
-    )(far_coefs, faces[2], part)
+        name="far",
+    )(far_coefs, chain_plane, part)
     mine = mine + lax.ppermute(twin, "dom", pairs)
     parts = lax.all_to_all(jnp.broadcast_to(mine, (count,) + mine.shape), "dom", 0, 0)
     scale = 3.0 * count * rows_y * cols_z

time: 44.4 us -> 42.6 us (0.959)
  Pallas kernels: 12.9 us -> 8.29 us
  waiting for transfers between devices: 1.16 us -> 5.23 us
  starting transfers between devices: 12.6 us -> 10.9 us
    ppermute x3 -> x1, starting transfers between devices: 12 us -> 6.59 us  [shards(): chain_plane = lax.ppermute(own, 'dom', chain)]
    ppermute x3 -> x1, waiting for transfers between devices: 0.01 us -> 4.4 us  [shards(): chain_plane = lax.ppermute(own, 'dom', chain)]
    ppermute x1, starting transfers between devices: 0.07 us -> 3.84 us  [shards(): mine = mine + lax.ppermute(twin, 'dom', pairs)]
    pallas_call x3 -> x1, Pallas kernels: 5.71 us -> 2.35 us  [shards(): pl.pallas_call(far_kernel, out_shape=(jax.ShapeDtypeStruct((3 * rows_y //...]
    slice x1 -> x0, local copies, waits for them, and re-layouts: 1.16 us -> none  [shards(): faces = [lax.ppermute(own[b:b + 1], 'dom', chain) for b in range(3)]]
    unnamed x4, local copies, waits for them, and re-layouts: 1.21 us -> 2.34 us
    pallas_call x1, Pallas kernels: 3.86 us -> 3.24 us  [shards(): pl.pallas_call(near_kernel, out_shape=(jax.ShapeDtypeStruct(own.shape, jn...]
    pallas_call x1, Pallas kernels: 3.31 us -> 2.7 us  [shards(): pl.pallas_call(functools.partial(basis_kernel, scale=scale), out_shape=(j...]
  transfers between devices with their start and end apart: 5 -> 3, of which waited for: 1 -> 2; matrix products, arithmetic and copies ran while one was open for 3% -> 0% of each run, Pallas kernels for 16% -> 8%
where the time goes in v3:
time: 42.6 us; the launch traced here: 42.4 us
  blocking collectives  14.8 us (35%)
  starting transfers between devices  10.9 us (26%)
  Pallas kernels  8.29 us (19%)
  waiting for transfers between devices  5.23 us (12%)
  local copies, waits for them, and re-layouts  2.42 us (6%)
  between operations  0.66 us (2%)
    all_to_all x1, blocking collectives, shards(): lax.all_to_all(jnp.broadcast_to(mine, (count,) + mine.shape), 'dom', 0, 0)  14.8 us
    ppermute x1, starting transfers between devices, shards(): chain_plane = lax.ppermute(own, 'dom', chain)  6.59 us
    ppermute x1, waiting for transfers between devices, shards(): chain_plane = lax.ppermute(own, 'dom', chain)  4.4 us
    ppermute x1, starting transfers between devices, shards(): mine = mine + lax.ppermute(twin, 'dom', pairs)  3.84 us
    pallas_call x1, Pallas kernels, shards(): pl.pallas_call(near_kernel, out_shape=(jax.ShapeDtypeStruct(own.shape, jn...  3.24 us
    pallas_call x1, Pallas kernels, shards(): pl.pallas_call(functools.partial(basis_kernel, scale=scale), out_shape=(j...  2.7 us
    pallas_call x1, Pallas kernels, shards(): pl.pallas_call(far_kernel, out_shape=(jax.ShapeDtypeStruct((3 * rows_y //...  2.35 us
    unnamed x4, local copies, waits for them, and re-layouts  2.34 us
  transfers between devices with their start and end apart: 3, of which 2 were waited for; matrix products, arithmetic and copies ran while one was open for 0% of the time, Pallas kernels for 8%

profile of v3, /device:TPU:0, one launch (start us, length us, event | category | flops | bytes accessed | tf_op | source)
XLA Modules:
  0.0 42.4 jit_solution(10847079965525692796)
XLA Ops:
  0.6 0.5 %collective-permute-start = (f32[3,64,8,128]{3,2,1,0:T(8,128)}, f32[3,64,8,128]{3,2,1,0:T(8,128)S(1)}, u32[]{:S(2)}, u32[]{:S(2)}) collective-permute-start(f32[3,64,8,128]{3,2,1,0:T(8,128)} %bitcast.4), channel_id=1, source_target_pairs={{0,1},{1,0},{2,3},{3,2},{4,5},{5,4},{6,7},{7,6},{8,9},{9,8},{10,11... | collective-permute-start | bytes 2359304 | tf_op jit(solution)/shard_map/ppermute | solution.py:295
  1.1 6.6 %collective-permute-start.1 = (f32[3,64,8,128]{3,2,1,0:T(8,128)}, f32[3,64,8,128]{3,2,1,0:T(8,128)S(1)}, u32[]{:S(2)}, u32[]{:S(2)}) collective-permute-start(f32[3,64,8,128]{3,2,1,0:T(8,128)} %bitcast.5), channel_id=1, source_target_pairs={{1,2},{3,4},{5,6},{7,8},{9,10},{11,12},{13,14},{15,16},{17,18},{19... | collective-permute-start | bytes 2359304 | tf_op jit(solution)/shard_map/ppermute | solution.py:293
  7.7 0.0 collective-permute-done.pair_ref
  7.7 0.0 copy-start
  7.7 1.2 %copy-done = f32[1,27,3,3,8,128]{5,4,3,2,1,0:T(8,128)S(1)} copy-done((f32[1,27,3,3,8,128]{5,4,3,2,1,0:T(8,128)S(1)}, f32[1,27,3,3,8,128]{5,4,3,2,1,0:T(8,128)}, u32[]{:S(2)}) %copy-start) | copy-done | bytes 995352
  9.0 0.0 copy-start.1
  9.0 1.1 %copy-done.1 = f32[1,3,64,8,128]{4,3,2,1,0:T(8,128)S(1)} copy-done((f32[1,3,64,8,128]{4,3,2,1,0:T(8,128)S(1)}, f32[1,3,64,8,128]{4,3,2,1,0:T(8,128)}, u32[]{:S(2)}) %copy-start.1) | copy-done | bytes 786456
  10.1 3.2 %near.1 = (f32[3,64,8,128]{3,2,1,0:T(8,128)S(1)}, f32[9,3,3,8,128]{4,3,2,1,0:T(8,128)S(1)}) custom-call(f32[27,3,3,8,128]{4,3,2,1,0:T(8,128)S(1)} %bitcast.3, f32[3,64,8,128]{3,2,1,0:T(8,128)S(1)} %bitcast.6, f32[3,64,8,128]{3,2,1,0:T(8,128)S(1)} %collective-permute-done.pair_ref), custom_call_target="tpu_custom_call" | custom-call | flops 21233664 | bytes 3932160 | tf_op jit(solution)/shard_map/near/pallas_call | solution.py:296
  13.3 4.4 %collective-permute-done.1.chain_ref = f32[3,64,8,128]{3,2,1,0:T(8,128)S(1)} collective-permute-done((f32[3,64,8,128]{3,2,1,0:T(8,128)}, f32[3,64,8,128]{3,2,1,0:T(8,128)S(1)}, u32[]{:S(2)}, u32[]{:S(2)}) %collective-permute-start.1) | collective-permute-done | bytes 786464 | tf_op jit(solution)/shard_map/ppermute | solution.py:293
  17.7 2.3 %far.1 = (bf16[12,128,256]{2,1,0:T(8,128)(2,1)S(1)}, f32[1,1152]{1,0:T(1,128)S(1)}, f32[1,1152]{1,0:T(1,128)S(1)}) custom-call(f32[9,3,3,8,128]{4,3,2,1,0:T(8,128)S(1)} %get-tuple-element.9.far_coef_ref, f32[3,64,8,128]{3,2,1,0:T(8,128)S(1)} %collective-permute-done.1.chain_ref, f32[3,64,8,128]{3,2,1,0:T(8,128)S(1)} %get-tuple-element.10.part_ref), custom_call_target="tpu_custom_call" | custom-call | tf_op jit(solution)/shard_map/far/pallas_call | solution.py:312
  20.1 3.8 %collective-permute-start.2 = (f32[1,1152]{1,0:T(1,128)S(1)}, f32[1,1152]{1,0:T(1,128)S(1)}, u32[]{:S(2)}, u32[]{:S(2)}) collective-permute-start(f32[1,1152]{1,0:T(1,128)S(1)} %get-tuple-element.12), channel_id=1, source_target_pairs={{0,1},{1,0},{2,3},{3,2},{4,5},{5,4},{6,7},{7,6},{8,9},{9,8},{10,11... | collective-permute-start | bytes 13832 | tf_op jit(solution)/shard_map/ppermute | solution.py:325
  23.9 0.8 %collective-permute-done.2 = f32[1,1152]{1,0:T(1,128)S(1)} collective-permute-done((f32[1,1152]{1,0:T(1,128)S(1)}, f32[1,1152]{1,0:T(1,128)S(1)}, u32[]{:S(2)}, u32[]{:S(2)}) %collective-permute-start.2) | collective-permute-done | bytes 4640 | tf_op jit(solution)/shard_map/ppermute | solution.py:325
  24.8 0.1 broadcast_in_dim.3
  24.9 14.8 %all_to_all.5.parts_ref = f32[32,1,1152]{2,1,0:T(1,128)S(1)} all-to-all(f32[32,1,1152]{2,1,0:T(1,128)S(1)} %broadcast_in_dim.3), channel_id=1, replica_groups=mesh['dom'=32] {'dom'}, dimensions={0} | all-to-all | bytes 294912 | tf_op jit(solution)/shard_map/all_to_all | solution.py:326
  39.7 2.7 %basis.1 = (f32[3,512,128]{2,1,0:T(8,128)}, f32[64,64]{1,0:T(8,128)}) custom-call(f32[32,1,1152]{2,1,0:T(1,128)S(1)} %all_to_all.5.parts_ref, bf16[12,128,256]{2,1,0:T(8,128)(2,1)S(1)} %get-tuple-element.13.split_ref), custom_call_target="tpu_custom_call" | custom-call | tf_op jit(solution)/shard_map/basis/pallas_call | solution.py:328
  (1 shorter events, 0.0 us)
Async XLA Ops:
  0.6 7.1 %collective-permute-start = (f32[3,64,8,128]{3,2,1,0:T(8,128)}, f32[3,64,8,128]{3,2,1,0:T(8,128)S(1)}, u32[]{:S(2)}, u32[]{:S(2)}) collective-permute-start(f32[3,64,8,128]{3,2,1,0:T(8,128)} %bitcast.4), channel_id=1, source_target_pairs={{0,1},{1,0},{2,3},{3,2},{4,5},{5,4},{6,7},{7,6},{8,9},{9,8},{10,11... | collective-permute-start | bytes 2359304 | tf_op jit(solution)/shard_map/ppermute | solution.py:295
  1.1 16.6 %collective-permute-start.1 = (f32[3,64,8,128]{3,2,1,0:T(8,128)}, f32[3,64,8,128]{3,2,1,0:T(8,128)S(1)}, u32[]{:S(2)}, u32[]{:S(2)}) collective-permute-start(f32[3,64,8,128]{3,2,1,0:T(8,128)} %bitcast.5), channel_id=1, source_target_pairs={{1,2},{3,4},{5,6},{7,8},{9,10},{11,12},{13,14},{15,16},{17,18},{19... | collective-permute-start | bytes 2359304 | tf_op jit(solution)/shard_map/ppermute | solution.py:293
  7.7 1.2 %copy-start = (f32[1,27,3,3,8,128]{5,4,3,2,1,0:T(8,128)S(1)}, f32[1,27,3,3,8,128]{5,4,3,2,1,0:T(8,128)}, u32[]{:S(2)}) copy-start(f32[1,27,3,3,8,128]{5,4,3,2,1,0:T(8,128)} %param.2) | copy-start | bytes 2985988
  9.0 1.1 %copy-start.1 = (f32[1,3,64,8,128]{4,3,2,1,0:T(8,128)S(1)}, f32[1,3,64,8,128]{4,3,2,1,0:T(8,128)}, u32[]{:S(2)}) copy-start(f32[1,3,64,8,128]{4,3,2,1,0:T(8,128)} %param.3) | copy-start | bytes 2359300
  20.1 4.7 %collective-permute-start.2 = (f32[1,1152]{1,0:T(1,128)S(1)}, f32[1,1152]{1,0:T(1,128)S(1)}, u32[]{:S(2)}, u32[]{:S(2)}) collective-permute-start(f32[1,1152]{1,0:T(1,128)S(1)} %get-tuple-element.12), channel_id=1, source_target_pairs={{0,1},{1,0},{2,3},{3,2},{4,5},{5,4},{6,7},{7,6},{8,9},{9,8},{10,11... | collective-permute-start | bytes 13832 | tf_op jit(solution)/shard_map/ppermute | solution.py:325

commit v4 on v3

--- a/solution.py
+++ b/solution.py
@@ -8,7 +8,7 @@
 from jax.sharding import PartitionSpec as P
 
 GROUP = 4
-UNROLL = 4
+UNROLL = 8
 VMEM_LIMIT = 48 * 1024 * 1024
 
 
@@ -165,24 +165,26 @@
     rows = []
     for r in range(9):
         x = parts_ref[:, 0, r * width : (r + 1) * width]
-        x = jnp.sum(x.reshape(x.shape[0] // 8, 8, width), axis=0)
+        x = jnp.sum(x.reshape(2, x.shape[0] // 16, 8, width), axis=1)
+        x = jnp.where(sub8 < 4, x[0] + pltpu.roll(x[0], 4, 0), x[1] + pltpu.roll(x[1], 4, 0))
         x = x + pltpu.roll(x, 2, 0)
-        rows.append(x + pltpu.roll(x, 4, 0))
+        rows.append(x + pltpu.roll(x, 1, 0))
     lane = iota((quarter, width), 1)
     sub = iota((quarter, width), 0)
     out = []
     for half in range(2):
+        at = 4 * half + 3
         body = jnp.zeros((8, width), jnp.float32)
         for r in range(8):
             body = jnp.where(
-                sub8 == r, jnp.broadcast_to(rows[r][half : half + 1], (8, width)), body
+                sub8 == r, jnp.broadcast_to(rows[r][at : at + 1], (8, width)), body
             )
         packed = jnp.concatenate([body, pltpu.roll(body, columns, 1)], axis=0)
         base = half * 2 * quarter
         upper = jnp.where(lane >= sub, packed, 0.0)
         upper = jnp.where(lane < 2 * quarter, upper, 0.0)
         lower = jnp.where(lane < sub, packed, 0.0)
-        diag = jnp.broadcast_to(rows[8][half : half + 1], (quarter, width))
+        diag = jnp.broadcast_to(rows[8][at : at + 1], (quarter, width))
         lower = jnp.where(lane == sub, diag, lower)
         lower = jnp.where(lane < quarter, lower, 0.0)
         cross = jnp.where((lane >= 2 * quarter) & (lane < columns), packed, 0.0)
@@ -323,7 +325,10 @@
         name="far",
     )(far_coefs, chain_plane, part)
     mine = mine + lax.ppermute(twin, "dom", pairs)
-    parts = lax.all_to_all(jnp.broadcast_to(mine, (count,) + mine.shape), "dom", 0, 0)
+    order = [*range(0, count, 2), *range(1, count, 2)]
+    parts = lax.all_to_all(
+        jnp.broadcast_to(mine, (count,) + mine.shape), "dom", 0, 0, axis_index_groups=[order]
+    )
     scale = 3.0 * count * rows_y * cols_z
     basis, factor = pl.pallas_call(
         functools.partial(basis_kernel, scale=scale),

time: 42.6 us -> 42.2 us (level)
  transfers between devices with their start and end apart: 3 -> 3, of which waited for: 2 -> 2; matrix products, arithmetic and copies ran while one was open for 0% -> 0% of each run, Pallas kernels for 8% -> 7%
where the time goes in v4:
time: 42.2 us; the launch traced here: 42 us
  blocking collectives  14.6 us (35%)
  starting transfers between devices  10.9 us (26%)
  Pallas kernels  8.01 us (19%)
  waiting for transfers between devices  5.37 us (13%)
  local copies, waits for them, and re-layouts  2.42 us (6%)
  between operations  0.66 us (2%)
    all_to_all x1, blocking collectives, shards(): lax.all_to_all(jnp.broadcast_to(mine, (count,) + mine.shape), 'dom', 0, 0...  14.6 us
    ppermute x1, starting transfers between devices, shards(): chain_plane = lax.ppermute(own, 'dom', chain)  6.59 us
    ppermute x1, waiting for transfers between devices, shards(): chain_plane = lax.ppermute(own, 'dom', chain)  4.54 us
    ppermute x1, starting transfers between devices, shards(): mine = mine + lax.ppermute(twin, 'dom', pairs)  3.83 us
    pallas_call x1, Pallas kernels, shards(): pl.pallas_call(near_kernel, out_shape=(jax.ShapeDtypeStruct(own.shape, jn...  3.1 us
    pallas_call x1, Pallas kernels, shards(): pl.pallas_call(functools.partial(basis_kernel, scale=scale), out_shape=(j...  2.71 us
    unnamed x4, local copies, waits for them, and re-layouts  2.34 us
    pallas_call x1, Pallas kernels, shards(): pl.pallas_call(far_kernel, out_shape=(jax.ShapeDtypeStruct((3 * rows_y //...  2.2 us
  transfers between devices with their start and end apart: 3, of which 2 were waited for; matrix products, arithmetic and copies ran while one was open for 0% of the time, Pallas kernels for 7%

profile of v4, /device:TPU:0, one launch (start us, length us, event | category | flops | bytes accessed | tf_op | source)
XLA Modules:
  0.0 42.0 jit_solution(9387775057197080761)
XLA Ops:
  0.6 0.5 %collective-permute-start = (f32[3,64,8,128]{3,2,1,0:T(8,128)}, f32[3,64,8,128]{3,2,1,0:T(8,128)S(1)}, u32[]{:S(2)}, u32[]{:S(2)}) collective-permute-start(f32[3,64,8,128]{3,2,1,0:T(8,128)} %bitcast.4), channel_id=1, source_target_pairs={{0,1},{1,0},{2,3},{3,2},{4,5},{5,4},{6,7},{7,6},{8,9},{9,8},{10,11... | collective-permute-start | bytes 2359304 | tf_op jit(solution)/shard_map/ppermute | solution.py:297
  1.1 6.6 %collective-permute-start.1 = (f32[3,64,8,128]{3,2,1,0:T(8,128)}, f32[3,64,8,128]{3,2,1,0:T(8,128)S(1)}, u32[]{:S(2)}, u32[]{:S(2)}) collective-permute-start(f32[3,64,8,128]{3,2,1,0:T(8,128)} %bitcast.5), channel_id=1, source_target_pairs={{1,2},{3,4},{5,6},{7,8},{9,10},{11,12},{13,14},{15,16},{17,18},{19... | collective-permute-start | bytes 2359304 | tf_op jit(solution)/shard_map/ppermute | solution.py:295
  7.7 0.0 collective-permute-done.pair_ref
  7.7 0.0 copy-start
  7.7 1.2 %copy-done = f32[1,27,3,3,8,128]{5,4,3,2,1,0:T(8,128)S(1)} copy-done((f32[1,27,3,3,8,128]{5,4,3,2,1,0:T(8,128)S(1)}, f32[1,27,3,3,8,128]{5,4,3,2,1,0:T(8,128)}, u32[]{:S(2)}) %copy-start) | copy-done | bytes 995352
  9.0 0.0 copy-start.1
  9.0 1.1 %copy-done.1 = f32[1,3,64,8,128]{4,3,2,1,0:T(8,128)S(1)} copy-done((f32[1,3,64,8,128]{4,3,2,1,0:T(8,128)S(1)}, f32[1,3,64,8,128]{4,3,2,1,0:T(8,128)}, u32[]{:S(2)}) %copy-start.1) | copy-done | bytes 786456
  10.1 3.1 %near.1 = (f32[3,64,8,128]{3,2,1,0:T(8,128)S(1)}, f32[9,3,3,8,128]{4,3,2,1,0:T(8,128)S(1)}) custom-call(f32[27,3,3,8,128]{4,3,2,1,0:T(8,128)S(1)} %bitcast.3, f32[3,64,8,128]{3,2,1,0:T(8,128)S(1)} %bitcast.6, f32[3,64,8,128]{3,2,1,0:T(8,128)S(1)} %collective-permute-done.pair_ref), custom_call_target="tpu_custom_call" | custom-call | flops 21233664 | bytes 3932160 | tf_op jit(solution)/shard_map/near/pallas_call | solution.py:298
  13.2 4.5 %collective-permute-done.1.chain_ref = f32[3,64,8,128]{3,2,1,0:T(8,128)S(1)} collective-permute-done((f32[3,64,8,128]{3,2,1,0:T(8,128)}, f32[3,64,8,128]{3,2,1,0:T(8,128)S(1)}, u32[]{:S(2)}, u32[]{:S(2)}) %collective-permute-start.1) | collective-permute-done | bytes 786464 | tf_op jit(solution)/shard_map/ppermute | solution.py:295
  17.7 2.2 %far.1 = (bf16[12,128,256]{2,1,0:T(8,128)(2,1)S(1)}, f32[1,1152]{1,0:T(1,128)S(1)}, f32[1,1152]{1,0:T(1,128)S(1)}) custom-call(f32[9,3,3,8,128]{4,3,2,1,0:T(8,128)S(1)} %get-tuple-element.9.far_coef_ref, f32[3,64,8,128]{3,2,1,0:T(8,128)S(1)} %collective-permute-done.1.chain_ref, f32[3,64,8,128]{3,2,1,0:T(8,128)S(1)} %get-tuple-element.10.part_ref), custom_call_target="tpu_custom_call" | custom-call | tf_op jit(solution)/shard_map/far/pallas_call | solution.py:314
  19.9 3.8 %collective-permute-start.2 = (f32[1,1152]{1,0:T(1,128)S(1)}, f32[1,1152]{1,0:T(1,128)S(1)}, u32[]{:S(2)}, u32[]{:S(2)}) collective-permute-start(f32[1,1152]{1,0:T(1,128)S(1)} %get-tuple-element.12), channel_id=1, source_target_pairs={{0,1},{1,0},{2,3},{3,2},{4,5},{5,4},{6,7},{7,6},{8,9},{9,8},{10,11... | collective-permute-start | bytes 13832 | tf_op jit(solution)/shard_map/ppermute | solution.py:327
  23.8 0.8 %collective-permute-done.2 = f32[1,1152]{1,0:T(1,128)S(1)} collective-permute-done((f32[1,1152]{1,0:T(1,128)S(1)}, f32[1,1152]{1,0:T(1,128)S(1)}, u32[]{:S(2)}, u32[]{:S(2)}) %collective-permute-start.2) | collective-permute-done | bytes 4640 | tf_op jit(solution)/shard_map/ppermute | solution.py:327
  24.6 0.1 broadcast_in_dim.3
  24.7 14.6 %all_to_all.5.parts_ref = f32[32,1,1152]{2,1,0:T(1,128)S(1)} all-to-all(f32[32,1,1152]{2,1,0:T(1,128)S(1)} %broadcast_in_dim.3), channel_id=1, replica_groups={{0,2,4,6,8,10,12,14,16,18,20,22,24,26,28,30,1,3,5,7,9,11,13,15,17,19,21..., dimensions={0} | all-to-all | bytes 294912 | tf_op jit(solution)/shard_map/all_to_all | solution.py:329
  39.3 2.7 %basis.1 = (f32[3,512,128]{2,1,0:T(8,128)}, f32[64,64]{1,0:T(8,128)}) custom-call(f32[32,1,1152]{2,1,0:T(1,128)S(1)} %all_to_all.5.parts_ref, bf16[12,128,256]{2,1,0:T(8,128)(2,1)S(1)} %get-tuple-element.13.split_ref), custom_call_target="tpu_custom_call" | custom-call | tf_op jit(solution)/shard_map/basis/pallas_call | solution.py:333
  (1 shorter events, 0.0 us)
Async XLA Ops:
  0.6 7.1 %collective-permute-start = (f32[3,64,8,128]{3,2,1,0:T(8,128)}, f32[3,64,8,128]{3,2,1,0:T(8,128)S(1)}, u32[]{:S(2)}, u32[]{:S(2)}) collective-permute-start(f32[3,64,8,128]{3,2,1,0:T(8,128)} %bitcast.4), channel_id=1, source_target_pairs={{0,1},{1,0},{2,3},{3,2},{4,5},{5,4},{6,7},{7,6},{8,9},{9,8},{10,11... | collective-permute-start | bytes 2359304 | tf_op jit(solution)/shard_map/ppermute | solution.py:297
  1.1 16.6 %collective-permute-start.1 = (f32[3,64,8,128]{3,2,1,0:T(8,128)}, f32[3,64,8,128]{3,2,1,0:T(8,128)S(1)}, u32[]{:S(2)}, u32[]{:S(2)}) collective-permute-start(f32[3,64,8,128]{3,2,1,0:T(8,128)} %bitcast.5), channel_id=1, source_target_pairs={{1,2},{3,4},{5,6},{7,8},{9,10},{11,12},{13,14},{15,16},{17,18},{19... | collective-permute-start | bytes 2359304 | tf_op jit(solution)/shard_map/ppermute | solution.py:295
  7.7 1.2 %copy-start = (f32[1,27,3,3,8,128]{5,4,3,2,1,0:T(8,128)S(1)}, f32[1,27,3,3,8,128]{5,4,3,2,1,0:T(8,128)}, u32[]{:S(2)}) copy-start(f32[1,27,3,3,8,128]{5,4,3,2,1,0:T(8,128)} %param.2) | copy-start | bytes 2985988
  9.0 1.1 %copy-start.1 = (f32[1,3,64,8,128]{4,3,2,1,0:T(8,128)S(1)}, f32[1,3,64,8,128]{4,3,2,1,0:T(8,128)}, u32[]{:S(2)}) copy-start(f32[1,3,64,8,128]{4,3,2,1,0:T(8,128)} %param.3) | copy-start | bytes 2359300
  19.9 4.7 %collective-permute-start.2 = (f32[1,1152]{1,0:T(1,128)S(1)}, f32[1,1152]{1,0:T(1,128)S(1)}, u32[]{:S(2)}, u32[]{:S(2)}) collective-permute-start(f32[1,1152]{1,0:T(1,128)S(1)} %get-tuple-element.12), channel_id=1, source_target_pairs={{0,1},{1,0},{2,3},{3,2},{4,5},{5,4},{6,7},{7,6},{8,9},{9,8},{10,11... | collective-permute-start | bytes 13832 | tf_op jit(solution)/shard_map/ppermute | solution.py:327

commit v5 on v4

--- a/solution.py
+++ b/solution.py
@@ -56,8 +56,9 @@
 
 def contract(coef_ref, parts, start, initial):
     rows_y, cols_z = coef_ref.shape[3:]
-    zero = jnp.zeros((GROUP, rows_y, cols_z), jnp.float32)
-    acc = [[zero for _ in range(3)] for _ in range(3)]
+    acc = [[None] * 3, [None] * 3, [None] * 3]
+    if initial is not None:
+        acc[1] = [initial[a, pl.ds(start, GROUP)] for a in range(3)]
     for sketch_ref, slot, b, first in parts:
         own = sketch_ref[slot, pl.ds(start, GROUP)]
         for dz in range(3):
@@ -68,14 +69,12 @@
                 moved = pltpu.roll(own, cols_z - 1, 2)
             for dy in range(3):
                 for a in range(3):
-                    acc[dy][a] += coef_ref[first + dy * 3 + dz, a, b][None] * moved
-    out = []
-    for a in range(3):
-        total = acc[1][a] + pltpu.roll(acc[0][a], 1, 1) + pltpu.roll(acc[2][a], rows_y - 1, 1)
-        if initial is not None:
-            total = total + initial[a, pl.ds(start, GROUP)]
-        out.append(total)
-    return out
+                    term = coef_ref[first + dy * 3 + dz, a, b][None] * moved
+                    acc[dy][a] = term if acc[dy][a] is None else acc[dy][a] + term
+    return [
+        acc[1][a] + pltpu.roll(acc[0][a], 1, 1) + pltpu.roll(acc[2][a], rows_y - 1, 1)
+        for a in range(3)
+    ]
 
 
 def near_kernel(coef_ref, own_ref, pair_ref, part_ref, far_coef_ref, work):
@@ -325,7 +324,7 @@
         name="far",
     )(far_coefs, chain_plane, part)
     mine = mine + lax.ppermute(twin, "dom", pairs)
-    order = [*range(0, count, 2), *range(1, count, 2)]
+    order = [*range(count // 2, count, 2), *range(0, count // 2, 2), *range(count // 2 + 1, count, 2), *range(1, count // 2, 2)]
     parts = lax.all_to_all(
         jnp.broadcast_to(mine, (count,) + mine.shape), "dom", 0, 0, axis_index_groups=[order]
     )

time: 42.2 us -> 42 us (level)
  no operation moved by 1% of the time
where the time goes in v5:
time: 42 us; the launch traced here: 41.8 us
  blocking collectives  14.4 us (34%)
  starting transfers between devices  10.9 us (26%)
  Pallas kernels  8.01 us (19%)
  waiting for transfers between devices  5.37 us (13%)
  local copies, waits for them, and re-layouts  2.42 us (6%)
  between operations  0.66 us (2%)
    all_to_all x1, blocking collectives, shards(): lax.all_to_all(jnp.broadcast_to(mine, (count,) + mine.shape), 'dom', 0, 0...  14.4 us
    ppermute x1, starting transfers between devices, shards(): chain_plane = lax.ppermute(own, 'dom', chain)  6.59 us
    ppermute x1, waiting for transfers between devices, shards(): chain_plane = lax.ppermute(own, 'dom', chain)  4.54 us
    ppermute x1, starting transfers between devices, shards(): mine = mine + lax.ppermute(twin, 'dom', pairs)  3.83 us
    pallas_call x1, Pallas kernels, shards(): pl.pallas_call(near_kernel, out_shape=(jax.ShapeDtypeStruct(own.shape, jn...  3.1 us
    pallas_call x1, Pallas kernels, shards(): pl.pallas_call(functools.partial(basis_kernel, scale=scale), out_shape=(j...  2.71 us
    unnamed x4, local copies, waits for them, and re-layouts  2.34 us
    pallas_call x1, Pallas kernels, shards(): pl.pallas_call(far_kernel, out_shape=(jax.ShapeDtypeStruct((3 * rows_y //...  2.2 us
  transfers between devices with their start and end apart: 3, of which 2 were waited for; matrix products, arithmetic and copies ran while one was open for 0% of the time, Pallas kernels for 7%

profile of v5, /device:TPU:0, one launch (start us, length us, event | category | flops | bytes accessed | tf_op | source)
XLA Modules:
  0.0 41.8 jit_solution(3361441488272745192)
XLA Ops:
  0.6 0.5 %collective-permute-start = (f32[3,64,8,128]{3,2,1,0:T(8,128)}, f32[3,64,8,128]{3,2,1,0:T(8,128)S(1)}, u32[]{:S(2)}, u32[]{:S(2)}) collective-permute-start(f32[3,64,8,128]{3,2,1,0:T(8,128)} %bitcast.4), channel_id=1, source_target_pairs={{0,1},{1,0},{2,3},{3,2},{4,5},{5,4},{6,7},{7,6},{8,9},{9,8},{10,11... | collective-permute-start | bytes 2359304 | tf_op jit(solution)/shard_map/ppermute | solution.py:296
  1.1 6.6 %collective-permute-start.1 = (f32[3,64,8,128]{3,2,1,0:T(8,128)}, f32[3,64,8,128]{3,2,1,0:T(8,128)S(1)}, u32[]{:S(2)}, u32[]{:S(2)}) collective-permute-start(f32[3,64,8,128]{3,2,1,0:T(8,128)} %bitcast.5), channel_id=1, source_target_pairs={{1,2},{3,4},{5,6},{7,8},{9,10},{11,12},{13,14},{15,16},{17,18},{19... | collective-permute-start | bytes 2359304 | tf_op jit(solution)/shard_map/ppermute | solution.py:294
  7.7 0.0 collective-permute-done.pair_ref
  7.7 0.0 copy-start
  7.7 1.2 %copy-done = f32[1,27,3,3,8,128]{5,4,3,2,1,0:T(8,128)S(1)} copy-done((f32[1,27,3,3,8,128]{5,4,3,2,1,0:T(8,128)S(1)}, f32[1,27,3,3,8,128]{5,4,3,2,1,0:T(8,128)}, u32[]{:S(2)}) %copy-start) | copy-done | bytes 995352
  9.0 0.0 copy-start.1
  9.0 1.1 %copy-done.1 = f32[1,3,64,8,128]{4,3,2,1,0:T(8,128)S(1)} copy-done((f32[1,3,64,8,128]{4,3,2,1,0:T(8,128)S(1)}, f32[1,3,64,8,128]{4,3,2,1,0:T(8,128)}, u32[]{:S(2)}) %copy-start.1) | copy-done | bytes 786456
  10.1 3.1 %near.1 = (f32[3,64,8,128]{3,2,1,0:T(8,128)S(1)}, f32[9,3,3,8,128]{4,3,2,1,0:T(8,128)S(1)}) custom-call(f32[27,3,3,8,128]{4,3,2,1,0:T(8,128)S(1)} %bitcast.3, f32[3,64,8,128]{3,2,1,0:T(8,128)S(1)} %bitcast.6, f32[3,64,8,128]{3,2,1,0:T(8,128)S(1)} %collective-permute-done.pair_ref), custom_call_target="tpu_custom_call" | custom-call | flops 21233664 | bytes 3932160 | tf_op jit(solution)/shard_map/near/pallas_call | solution.py:297
  13.2 4.5 %collective-permute-done.1.chain_ref = f32[3,64,8,128]{3,2,1,0:T(8,128)S(1)} collective-permute-done((f32[3,64,8,128]{3,2,1,0:T(8,128)}, f32[3,64,8,128]{3,2,1,0:T(8,128)S(1)}, u32[]{:S(2)}, u32[]{:S(2)}) %collective-permute-start.1) | collective-permute-done | bytes 786464 | tf_op jit(solution)/shard_map/ppermute | solution.py:294
  17.7 2.2 %far.1 = (bf16[12,128,256]{2,1,0:T(8,128)(2,1)S(1)}, f32[1,1152]{1,0:T(1,128)S(1)}, f32[1,1152]{1,0:T(1,128)S(1)}) custom-call(f32[9,3,3,8,128]{4,3,2,1,0:T(8,128)S(1)} %get-tuple-element.9.far_coef_ref, f32[3,64,8,128]{3,2,1,0:T(8,128)S(1)} %collective-permute-done.1.chain_ref, f32[3,64,8,128]{3,2,1,0:T(8,128)S(1)} %get-tuple-element.10.part_ref), custom_call_target="tpu_custom_call" | custom-call | tf_op jit(solution)/shard_map/far/pallas_call | solution.py:313
  19.9 3.8 %collective-permute-start.2 = (f32[1,1152]{1,0:T(1,128)S(1)}, f32[1,1152]{1,0:T(1,128)S(1)}, u32[]{:S(2)}, u32[]{:S(2)}) collective-permute-start(f32[1,1152]{1,0:T(1,128)S(1)} %get-tuple-element.12), channel_id=1, source_target_pairs={{0,1},{1,0},{2,3},{3,2},{4,5},{5,4},{6,7},{7,6},{8,9},{9,8},{10,11... | collective-permute-start | bytes 13832 | tf_op jit(solution)/shard_map/ppermute | solution.py:326
  23.8 0.8 %collective-permute-done.2 = f32[1,1152]{1,0:T(1,128)S(1)} collective-permute-done((f32[1,1152]{1,0:T(1,128)S(1)}, f32[1,1152]{1,0:T(1,128)S(1)}, u32[]{:S(2)}, u32[]{:S(2)}) %collective-permute-start.2) | collective-permute-done | bytes 4640 | tf_op jit(solution)/shard_map/ppermute | solution.py:326
  24.6 0.1 broadcast_in_dim.3
  24.7 14.4 %all_to_all.5.parts_ref = f32[32,1,1152]{2,1,0:T(1,128)S(1)} all-to-all(f32[32,1,1152]{2,1,0:T(1,128)S(1)} %broadcast_in_dim.3), channel_id=1, replica_groups={{16,18,20,22,24,26,28,30,0,2,4,6,8,10,12,14,17,19,21,23,25,27,29,31,1,3..., dimensions={0} | all-to-all | bytes 294912 | tf_op jit(solution)/shard_map/all_to_all | solution.py:328
  39.1 2.7 %basis.1 = (f32[3,512,128]{2,1,0:T(8,128)}, f32[64,64]{1,0:T(8,128)}) custom-call(f32[32,1,1152]{2,1,0:T(1,128)S(1)} %all_to_all.5.parts_ref, bf16[12,128,256]{2,1,0:T(8,128)(2,1)S(1)} %get-tuple-element.13.split_ref), custom_call_target="tpu_custom_call" | custom-call | tf_op jit(solution)/shard_map/basis/pallas_call | solution.py:332
  (1 shorter events, 0.0 us)
Async XLA Ops:
  0.6 7.1 %collective-permute-start = (f32[3,64,8,128]{3,2,1,0:T(8,128)}, f32[3,64,8,128]{3,2,1,0:T(8,128)S(1)}, u32[]{:S(2)}, u32[]{:S(2)}) collective-permute-start(f32[3,64,8,128]{3,2,1,0:T(8,128)} %bitcast.4), channel_id=1, source_target_pairs={{0,1},{1,0},{2,3},{3,2},{4,5},{5,4},{6,7},{7,6},{8,9},{9,8},{10,11... | collective-permute-start | bytes 2359304 | tf_op jit(solution)/shard_map/ppermute | solution.py:296
  1.1 16.6 %collective-permute-start.1 = (f32[3,64,8,128]{3,2,1,0:T(8,128)}, f32[3,64,8,128]{3,2,1,0:T(8,128)S(1)}, u32[]{:S(2)}, u32[]{:S(2)}) collective-permute-start(f32[3,64,8,128]{3,2,1,0:T(8,128)} %bitcast.5), channel_id=1, source_target_pairs={{1,2},{3,4},{5,6},{7,8},{9,10},{11,12},{13,14},{15,16},{17,18},{19... | collective-permute-start | bytes 2359304 | tf_op jit(solution)/shard_map/ppermute | solution.py:294
  7.7 1.2 %copy-start = (f32[1,27,3,3,8,128]{5,4,3,2,1,0:T(8,128)S(1)}, f32[1,27,3,3,8,128]{5,4,3,2,1,0:T(8,128)}, u32[]{:S(2)}) copy-start(f32[1,27,3,3,8,128]{5,4,3,2,1,0:T(8,128)} %param.2) | copy-start | bytes 2985988
  9.0 1.1 %copy-start.1 = (f32[1,3,64,8,128]{4,3,2,1,0:T(8,128)S(1)}, f32[1,3,64,8,128]{4,3,2,1,0:T(8,128)}, u32[]{:S(2)}) copy-start(f32[1,3,64,8,128]{4,3,2,1,0:T(8,128)} %param.3) | copy-start | bytes 2359300
  19.9 4.7 %collective-permute-start.2 = (f32[1,1152]{1,0:T(1,128)S(1)}, f32[1,1152]{1,0:T(1,128)S(1)}, u32[]{:S(2)}, u32[]{:S(2)}) collective-permute-start(f32[1,1152]{1,0:T(1,128)S(1)} %get-tuple-element.12), channel_id=1, source_target_pairs={{0,1},{1,0},{2,3},{3,2},{4,5},{5,4},{6,7},{7,6},{8,9},{9,8},{10,11... | collective-permute-start | bytes 13832 | tf_op jit(solution)/shard_map/ppermute | solution.py:326

commit v6 on v5

--- a/solution.py
+++ b/solution.py
@@ -7,8 +7,8 @@
 from jax.experimental.pallas import tpu as pltpu
 from jax.sharding import PartitionSpec as P
 
-GROUP = 4
-UNROLL = 8
+GROUP = 2
+UNROLL = 16
 VMEM_LIMIT = 48 * 1024 * 1024
 
 

time: 42 us -> 42 us (level)
  no operation moved by 1% of the time
where the time goes in v6:
time: 42 us; the launch traced here: 41.8 us
  blocking collectives  14.4 us (34%)
  starting transfers between devices  10.9 us (26%)
  Pallas kernels  7.97 us (19%)
  waiting for transfers between devices  5.39 us (13%)
  local copies, waits for them, and re-layouts  2.42 us (6%)
  between operations  0.66 us (2%)
    all_to_all x1, blocking collectives, shards(): lax.all_to_all(jnp.broadcast_to(mine, (count,) + mine.shape), 'dom', 0, 0...  14.4 us
    ppermute x1, starting transfers between devices, shards(): chain_plane = lax.ppermute(own, 'dom', chain)  6.59 us
    ppermute x1, waiting for transfers between devices, shards(): chain_plane = lax.ppermute(own, 'dom', chain)  4.56 us
    ppermute x1, starting transfers between devices, shards(): mine = mine + lax.ppermute(twin, 'dom', pairs)  3.83 us
    pallas_call x1, Pallas kernels, shards(): pl.pallas_call(near_kernel, out_shape=(jax.ShapeDtypeStruct(own.shape, jn...  3.08 us
    pallas_call x1, Pallas kernels, shards(): pl.pallas_call(functools.partial(basis_kernel, scale=scale), out_shape=(j...  2.71 us
    unnamed x4, local copies, waits for them, and re-layouts  2.34 us
    pallas_call x1, Pallas kernels, shards(): pl.pallas_call(far_kernel, out_shape=(jax.ShapeDtypeStruct((3 * rows_y //...  2.18 us
  transfers between devices with their start and end apart: 3, of which 2 were waited for; matrix products, arithmetic and copies ran while one was open for 0% of the time, Pallas kernels for 7%

profile of v6, /device:TPU:0, one launch (start us, length us, event | category | flops | bytes accessed | tf_op | source)
XLA Modules:
  0.0 41.8 jit_solution(6322199553932145069)
XLA Ops:
  0.6 0.5 %collective-permute-start = (f32[3,64,8,128]{3,2,1,0:T(8,128)}, f32[3,64,8,128]{3,2,1,0:T(8,128)S(1)}, u32[]{:S(2)}, u32[]{:S(2)}) collective-permute-start(f32[3,64,8,128]{3,2,1,0:T(8,128)} %bitcast.4), channel_id=1, source_target_pairs={{0,1},{1,0},{2,3},{3,2},{4,5},{5,4},{6,7},{7,6},{8,9},{9,8},{10,11... | collective-permute-start | bytes 2359304 | tf_op jit(solution)/shard_map/ppermute | solution.py:296
  1.1 6.6 %collective-permute-start.1 = (f32[3,64,8,128]{3,2,1,0:T(8,128)}, f32[3,64,8,128]{3,2,1,0:T(8,128)S(1)}, u32[]{:S(2)}, u32[]{:S(2)}) collective-permute-start(f32[3,64,8,128]{3,2,1,0:T(8,128)} %bitcast.5), channel_id=1, source_target_pairs={{1,2},{3,4},{5,6},{7,8},{9,10},{11,12},{13,14},{15,16},{17,18},{19... | collective-permute-start | bytes 2359304 | tf_op jit(solution)/shard_map/ppermute | solution.py:294
  7.7 0.0 collective-permute-done.pair_ref
  7.7 0.0 copy-start
  7.7 1.2 %copy-done = f32[1,27,3,3,8,128]{5,4,3,2,1,0:T(8,128)S(1)} copy-done((f32[1,27,3,3,8,128]{5,4,3,2,1,0:T(8,128)S(1)}, f32[1,27,3,3,8,128]{5,4,3,2,1,0:T(8,128)}, u32[]{:S(2)}) %copy-start) | copy-done | bytes 995352
  9.0 0.0 copy-start.1
  9.0 1.1 %copy-done.1 = f32[1,3,64,8,128]{4,3,2,1,0:T(8,128)S(1)} copy-done((f32[1,3,64,8,128]{4,3,2,1,0:T(8,128)S(1)}, f32[1,3,64,8,128]{4,3,2,1,0:T(8,128)}, u32[]{:S(2)}) %copy-start.1) | copy-done | bytes 786456
  10.1 3.1 %near.1 = (f32[3,64,8,128]{3,2,1,0:T(8,128)S(1)}, f32[9,3,3,8,128]{4,3,2,1,0:T(8,128)S(1)}) custom-call(f32[27,3,3,8,128]{4,3,2,1,0:T(8,128)S(1)} %bitcast.3, f32[3,64,8,128]{3,2,1,0:T(8,128)S(1)} %bitcast.6, f32[3,64,8,128]{3,2,1,0:T(8,128)S(1)} %collective-permute-done.pair_ref), custom_call_target="tpu_custom_call" | custom-call | flops 21233664 | bytes 3932160 | tf_op jit(solution)/shard_map/near/pallas_call | solution.py:297
  13.2 4.6 %collective-permute-done.1.chain_ref = f32[3,64,8,128]{3,2,1,0:T(8,128)S(1)} collective-permute-done((f32[3,64,8,128]{3,2,1,0:T(8,128)}, f32[3,64,8,128]{3,2,1,0:T(8,128)S(1)}, u32[]{:S(2)}, u32[]{:S(2)}) %collective-permute-start.1) | collective-permute-done | bytes 786464 | tf_op jit(solution)/shard_map/ppermute | solution.py:294
  17.7 2.2 %far.1 = (bf16[12,128,256]{2,1,0:T(8,128)(2,1)S(1)}, f32[1,1152]{1,0:T(1,128)S(1)}, f32[1,1152]{1,0:T(1,128)S(1)}) custom-call(f32[9,3,3,8,128]{4,3,2,1,0:T(8,128)S(1)} %get-tuple-element.9.far_coef_ref, f32[3,64,8,128]{3,2,1,0:T(8,128)S(1)} %collective-permute-done.1.chain_ref, f32[3,64,8,128]{3,2,1,0:T(8,128)S(1)} %get-tuple-element.10.part_ref), custom_call_target="tpu_custom_call" | custom-call | tf_op jit(solution)/shard_map/far/pallas_call | solution.py:313
  19.9 3.8 %collective-permute-start.2 = (f32[1,1152]{1,0:T(1,128)S(1)}, f32[1,1152]{1,0:T(1,128)S(1)}, u32[]{:S(2)}, u32[]{:S(2)}) collective-permute-start(f32[1,1152]{1,0:T(1,128)S(1)} %get-tuple-element.12), channel_id=1, source_target_pairs={{0,1},{1,0},{2,3},{3,2},{4,5},{5,4},{6,7},{7,6},{8,9},{9,8},{10,11... | collective-permute-start | bytes 13832 | tf_op jit(solution)/shard_map/ppermute | solution.py:326
  23.8 0.8 %collective-permute-done.2 = f32[1,1152]{1,0:T(1,128)S(1)} collective-permute-done((f32[1,1152]{1,0:T(1,128)S(1)}, f32[1,1152]{1,0:T(1,128)S(1)}, u32[]{:S(2)}, u32[]{:S(2)}) %collective-permute-start.2) | collective-permute-done | bytes 4640 | tf_op jit(solution)/shard_map/ppermute | solution.py:326
  24.6 0.1 broadcast_in_dim.3
  24.7 14.4 %all_to_all.5.parts_ref = f32[32,1,1152]{2,1,0:T(1,128)S(1)} all-to-all(f32[32,1,1152]{2,1,0:T(1,128)S(1)} %broadcast_in_dim.3), channel_id=1, replica_groups={{16,18,20,22,24,26,28,30,0,2,4,6,8,10,12,14,17,19,21,23,25,27,29,31,1,3..., dimensions={0} | all-to-all | bytes 294912 | tf_op jit(solution)/shard_map/all_to_all | solution.py:328
  39.1 2.7 %basis.1 = (f32[3,512,128]{2,1,0:T(8,128)}, f32[64,64]{1,0:T(8,128)}) custom-call(f32[32,1,1152]{2,1,0:T(1,128)S(1)} %all_to_all.5.parts_ref, bf16[12,128,256]{2,1,0:T(8,128)(2,1)S(1)} %get-tuple-element.13.split_ref), custom_call_target="tpu_custom_call" | custom-call | tf_op jit(solution)/shard_map/basis/pallas_call | solution.py:332
  (1 shorter events, 0.0 us)
Async XLA Ops:
  0.6 7.1 %collective-permute-start = (f32[3,64,8,128]{3,2,1,0:T(8,128)}, f32[3,64,8,128]{3,2,1,0:T(8,128)S(1)}, u32[]{:S(2)}, u32[]{:S(2)}) collective-permute-start(f32[3,64,8,128]{3,2,1,0:T(8,128)} %bitcast.4), channel_id=1, source_target_pairs={{0,1},{1,0},{2,3},{3,2},{4,5},{5,4},{6,7},{7,6},{8,9},{9,8},{10,11... | collective-permute-start | bytes 2359304 | tf_op jit(solution)/shard_map/ppermute | solution.py:296
  1.1 16.6 %collective-permute-start.1 = (f32[3,64,8,128]{3,2,1,0:T(8,128)}, f32[3,64,8,128]{3,2,1,0:T(8,128)S(1)}, u32[]{:S(2)}, u32[]{:S(2)}) collective-permute-start(f32[3,64,8,128]{3,2,1,0:T(8,128)} %bitcast.5), channel_id=1, source_target_pairs={{1,2},{3,4},{5,6},{7,8},{9,10},{11,12},{13,14},{15,16},{17,18},{19... | collective-permute-start | bytes 2359304 | tf_op jit(solution)/shard_map/ppermute | solution.py:294
  7.7 1.2 %copy-start = (f32[1,27,3,3,8,128]{5,4,3,2,1,0:T(8,128)S(1)}, f32[1,27,3,3,8,128]{5,4,3,2,1,0:T(8,128)}, u32[]{:S(2)}) copy-start(f32[1,27,3,3,8,128]{5,4,3,2,1,0:T(8,128)} %param.2) | copy-start | bytes 2985988
  9.0 1.1 %copy-start.1 = (f32[1,3,64,8,128]{4,3,2,1,0:T(8,128)S(1)}, f32[1,3,64,8,128]{4,3,2,1,0:T(8,128)}, u32[]{:S(2)}) copy-start(f32[1,3,64,8,128]{4,3,2,1,0:T(8,128)} %param.3) | copy-start | bytes 2359300
  19.9 4.7 %collective-permute-start.2 = (f32[1,1152]{1,0:T(1,128)S(1)}, f32[1,1152]{1,0:T(1,128)S(1)}, u32[]{:S(2)}, u32[]{:S(2)}) collective-permute-start(f32[1,1152]{1,0:T(1,128)S(1)} %get-tuple-element.12), channel_id=1, source_target_pairs={{0,1},{1,0},{2,3},{3,2},{4,5},{5,4},{6,7},{7,6},{8,9},{9,8},{10,11... | collective-permute-start | bytes 13832 | tf_op jit(solution)/shard_map/ppermute | solution.py:326
